TPU v7x, 512 devices: a whole 4x4x16 slice. The times are simulated.
512 devices in a mesh: dp: 16 (over x, y), seq: 32 (over z, core).
Axes of the slice: x: 4, y: 4, z: 16, core: 2. Of those that a mesh axis runs over, the one named last changes fastest.
Arguments:
- queries: bfloat16 [16, 4096, 768], P('dp', 'seq'), may hold values from -9 to 9
- keys: bfloat16 [16, 4096, 768], P('dp', 'seq'), may hold values from -9 to 9
- values: bfloat16 [16, 4096, 768], P('dp', 'seq'), may hold values from -6 to 6
- cotangent: bfloat16 [16, 4096, 768], P('dp', 'seq'), may hold values from -6 to 6
- pos_bias: float32 [768], replicated, may hold values from -3 to 3
- owner: int32 [16, 4096], P('dp', 'seq'), may hold values from 0 to 31, as said below
- slot: int32 [16, 4096], P('dp', 'seq'), may hold values from 0 to 127, as said below
- lengths: int32 [16, 4], P('dp'), may hold values from 1 to 2048, 4096 in all within a row
Outputs:
- attended: bfloat16 [16, 4096, 768], P('dp', 'seq')
- grad_queries: bfloat16 [16, 4096, 768], P('dp', 'seq')
- grad_keys: bfloat16 [16, 4096, 768], P('dp', 'seq')
- grad_values: bfloat16 [16, 4096, 768], P('dp', 'seq')
- grad_bias: float32 [768], replicated
Inputs may be any that keep to these rules, and one draw needn't show every extreme that they name: Per pack, owner * 128 + slot is a permutation of the pack's positions. The rows of one device (aligned blocks of 128) name any one owner at most 8 times, and in every pack some device names some owner exactly 8 times. `slot`: see owner.
All inputs are finite; a program needn't handle non-finite values.
Results may differ from a plain program's by a relative error of at most 0.017.
The roundings to bfloat16 on the way count: a program that leaves them out, or rounds other values in their place, can miss the bound.
Values may be sent and summed in bfloat16 or wider, within the bound.
A program may use at most 64 MiB of HBM per device.

v0:
```python
import jax
import jax.numpy as jnp
from jax import lax
from jax.sharding import PartitionSpec as P

HEAD_DIM = 64


def extended(value, sides, width):
    for axis, dim in sides:
        devices, length = (lax.axis_size(axis), value.shape[dim])
        up = [(i, (i + 1) % devices) for i in range(devices - 1)]
        down = [(j, i) for i, j in up]
        last = lax.slice_in_dim(value, length - width, length, axis=dim)
        initial = lax.slice_in_dim(value, 0, width, axis=dim)
        before = lax.ppermute(last, axis, up)
        after = lax.ppermute(initial, axis, down)
        value = jnp.concatenate([before, value, after], axis=dim)
    return value


def shifted(block, axis, distance):
    devices = range(lax.axis_size(axis))
    route = [(i - distance, i) for i in devices if i - distance in devices]
    return lax.ppermute(block, axis, route)


def head_forward(qh, kh, vh, mask):
    scale = 1.0 / jnp.sqrt(jnp.float32(qh.shape[-1]))
    s = (
        lax.dot_general(qh, kh, (((1,), (1,)), ((), ())), preferred_element_type=jnp.float32)
        * scale
    )
    s = jnp.where(mask, s, -1e30)
    top = jnp.max(s, axis=1)
    lse = top + jnp.log(jnp.sum(jnp.exp(s - top[:, None]), axis=1))
    p = jnp.where(mask, jnp.exp(s - lse[:, None]), 0.0)
    o = jnp.dot(p.astype(jnp.bfloat16), vh, preferred_element_type=jnp.float32).astype(jnp.bfloat16)
    return (o, lse)


def head_backward(qh, kh, vh, doh, oh, lse, mask):
    scale = 1.0 / jnp.sqrt(jnp.float32(qh.shape[-1]))
    s = (
        lax.dot_general(qh, kh, (((1,), (1,)), ((), ())), preferred_element_type=jnp.float32)
        * scale
    )
    p = jnp.where(mask, jnp.exp(s - lse[:, None]), 0.0)
    prob = p.astype(jnp.bfloat16)
    dpm = lax.dot_general(doh, vh, (((1,), (1,)), ((), ())), preferred_element_type=jnp.float32)
    delta = jnp.sum(doh.astype(jnp.float32) * oh.astype(jnp.float32), axis=1)
    ds = (p * (dpm - delta[:, None]) * scale).astype(jnp.bfloat16)
    dq = jnp.dot(ds, kh, preferred_element_type=jnp.float32)
    dkw = lax.dot_general(ds, qh, (((0,), (0,)), ((), ())), preferred_element_type=jnp.float32)
    dvw = lax.dot_general(prob, doh, (((0,), (0,)), ((), ())), preferred_element_type=jnp.float32)
    return (dq, dkw, dvw)


def body(queries, keys, values, cotangent, pos_bias, owner, slot, lengths):
    rows = queries.shape[1]
    width = queries.shape[2]
    heads = width // HEAD_DIM
    peers = lax.axis_size("seq")
    room = 2 * rows // peers
    here = lax.axis_index("seq")

    def heads_first(x):
        return x.reshape(x.shape[0], heads, HEAD_DIM).transpose(1, 0, 2)

    def heads_last(x):
        return x.transpose(1, 0, 2).reshape(x.shape[1], width)

    dest = owner[0]
    onehot = (dest[:, None] == jnp.arange(peers, dtype=jnp.int32)[None, :]).astype(jnp.int32)
    earlier = jnp.cumsum(onehot, 0) - onehot
    place = dest * room + jnp.sum(earlier * onehot, 1)
    marks = jnp.zeros((peers * room,), jnp.int32).at[place].set(slot[0] + 1).reshape(peers, room)
    marks = lax.all_to_all(marks, "seq", split_axis=0, concat_axis=0, tiled=True).reshape(
        peers * room
    )
    landing = jnp.where(marks > 0, marks - 1, rows)
    stack = jnp.stack([queries[0], keys[0], values[0], cotangent[0]], 1)
    buffer = jnp.zeros((peers * room,) + stack.shape[1:], jnp.bfloat16).at[place].set(stack)
    received = lax.all_to_all(
        buffer.reshape((peers, room) + stack.shape[1:]),
        "seq",
        split_axis=0,
        concat_axis=0,
        tiled=True,
    )
    flat = received.reshape((peers * room,) + received.shape[2:])
    arrived = jnp.zeros((rows,) + flat.shape[1:], jnp.bfloat16).at[landing].set(flat, mode="drop")
    q_arr = arrived[:, 0]
    k_arr = arrived[:, 1]
    v_arr = arrived[:, 2]
    frames = rows * peers
    start = here * rows
    own_pos = start + jnp.arange(rows, dtype=jnp.int32)
    win_pos = start - rows + jnp.arange(3 * rows, dtype=jnp.int32)
    ends = jnp.cumsum(lengths[0])
    seg_own = jnp.sum((own_pos[:, None] >= ends[None, :]).astype(jnp.int32), 1)
    seg_win = jnp.sum((win_pos[:, None] >= ends[None, :]).astype(jnp.int32), 1)
    inside = (win_pos >= 0) & (win_pos < frames)
    same = seg_own[:, None] == seg_win[None, :]
    near = jnp.abs(own_pos[:, None] - win_pos[None, :]) <= rows
    mask = near & same & inside[None, :]
    biased = (q_arr.astype(jnp.float32) + pos_bias[None, :]).astype(jnp.bfloat16)
    kv_win = extended(jnp.stack([k_arr, v_arr], 1), (("seq", 0),), rows)
    bq = heads_first(biased)
    bk = heads_first(kv_win[:, 0])
    bv = heads_first(kv_win[:, 1])
    o_h, lse_h = lax.map(lambda a: head_forward(a[0], a[1], a[2], mask), (bq, bk, bv))
    out_arr = heads_last(o_h)
    do_arr = arrived[:, 3]
    g_h = heads_first(do_arr)
    dq_h, dkw_h, dvw_h = lax.map(
        lambda a: head_backward(a[0], a[1], a[2], a[3], a[4], a[5], mask),
        (bq, bk, bv, g_h, o_h, lse_h),
    )
    dq_f = heads_last(dq_h)
    parts = jnp.stack([heads_last(dkw_h), heads_last(dvw_h)], 1)
    from_next = shifted(parts[:rows].astype(jnp.bfloat16), "seq", -1).astype(jnp.float32)
    from_prev = shifted(parts[2 * rows :].astype(jnp.bfloat16), "seq", 1).astype(jnp.float32)
    total = parts[rows : 2 * rows] + from_prev + from_next
    grads = jnp.stack(
        [
            dq_f.astype(jnp.bfloat16),
            total[:, 0].astype(jnp.bfloat16),
            total[:, 1].astype(jnp.bfloat16),
        ],
        1,
    )
    arranged = jnp.concatenate([out_arr[:, None], grads], 1)
    padded = jnp.concatenate([arranged, jnp.zeros((1,) + arranged.shape[1:], jnp.bfloat16)], 0)
    received = lax.all_to_all(
        padded[landing].reshape((peers, room) + arranged.shape[1:]),
        "seq",
        split_axis=0,
        concat_axis=0,
        tiled=True,
    )
    back = received.reshape((peers * room,) + received.shape[2:])[place]
    attended = back[:, 0]
    mine = back[:, 1:]
    grad_bias = lax.psum(jnp.sum(dq_f, 0), ("dp", "seq"))
    return (attended[None], mine[:, 0][None], mine[:, 1][None], mine[:, 2][None], grad_bias)


def solution(mesh):
    in_specs = (
        P("dp", "seq", None),
        P("dp", "seq", None),
        P("dp", "seq", None),
        P("dp", "seq", None),
        P(),
        P("dp", "seq"),
        P("dp", "seq"),
        P("dp", None),
    )
    out_specs = (
        P("dp", "seq", None),
        P("dp", "seq", None),
        P("dp", "seq", None),
        P("dp", "seq", None),
        P(),
    )
    return jax.shard_map(body, mesh=mesh, in_specs=in_specs, out_specs=out_specs, check_vma=False)
```

profile of v0, /device:TPU:1, one launch (start us, length us, event | category | flops | bytes accessed | tf_op | source)
XLA Modules:
  0.0 450.0 jit_solution(493685341384302930)
XLA Ops:
  5.4 16.8 %all-to-all-start = ((s32[32,1,8]{2,1,0:T(1,128)}), s32[32,1,8]{2,1,0:T(1,128)S(1)}, u32[]{:S(2)}, u32[]{:S(2)}) async-start(s32[32,1,8]{2,1,0:T(1,128)} %bitcast.5), calls=%async_computation | async-start | bytes 32768 | tf_op jit(solution)/shard_map/all_to_all | solution.py:78
  24.5 4.5 scatter_fusion
  30.4 3.4 all-to-all-done
  33.9 8.9 %all-to-all-start.1 = ((bf16[32,8,4,768]{3,1,2,0:T(8,128)(2,1)}), bf16[32,8,4,768]{3,1,2,0:T(8,128)(2,1)S(1)}, u32[]{:S(2)}, u32[]{:S(2)}) async-start(bf16[32,8,4,768]{3,1,2,0:T(8,128)(2,1)} %copy.103), calls=%async_computation.1 | async-start | bytes 3145728 | tf_op jit(solution)/shard_map/all_to_all | solution.py:84
  45.6 75.0 %all-to-all-done.1 = bf16[32,8,4,768]{3,1,2,0:T(8,128)(2,1)S(1)} async-done(((bf16[32,8,4,768]{3,1,2,0:T(8,128)(2,1)}), bf16[32,8,4,768]{3,1,2,0:T(8,128)(2,1)S(1)}, u32[]{:S(2)}, u32[]{:S(2)}) %all-to-all-start.1) | async-done | bytes 1572896 | tf_op jit(solution)/shard_map/all_to_all | solution.py:84
  122.1 7.6 %scatter_fusion.1 = bf16[128,4,768]{2,1,0:T(4,128)(2,1)S(1)} fusion(bf16[128,4,768]{2,1,0:T(4,128)(2,1)S(1)} %broadcast_in_dim.71, s32[256]{0:T(256)S(1)} %bitcast.176, bf16[256,4,768]{2,1,0:T(4,128)(2,1)S(1)} %copy.105), kind=kCustom, calls=%fused_computation.4 | custom fusion | bytes 4719616 | tf_op jit(solution)/shard_map/scatter | solution.py:92
  130.2 1.9 collective-permute-start
  132.1 2.6 collective-permute-start.1
  137.0 4.2 collective-permute-done.1
  141.2 1.7 pad_maximum_fusion.1
  144.5 1.7 copy.108
  147.0 1.7 copy.109
  149.5 49.0 %while.28 = (s32[]{:T(128)}, bf16[12,128,64]{1,2,0:T(8,128)(2,1)}, f32[12,128]{1,0:T(8,128)}, bf16[12,128,64]{2,1,0:T(8,128)(2,1)}, bf16[12,384,64]{2,1,0:T(8,12...) while((s32[]{:T(128)}, bf16[12,128,64]{1,2,0:T(8,128)(2,1)}, ...), condition=%wide.region_11.12_spmd.clone, body=%wide.region_8.11_spmd.clone.sunk | while | flops 13574018 | bytes 853633 | solution.py:112
  198.5 67.2 %while.29 = (s32[]{:T(128)}, f32[12,128,64]{1,2,0:T(8,128)S(1)}, f32[12,384,64]{1,2,0:T(8,128)}, f32[12,384,64]{1,2,0:T(8,128)}, bf16[12,128,64]{2,1,0:T(8,128)(...) while((s32[]{:T(128)}, f32[12,128,64]{1,2,0:T(8,128)S(1)}, ...), condition=%wide.region_14.15_spmd.clone, body=%wide.region_12.14_spmd.clone.sunk | while | flops 32178048 | bytes 1684637 | solution.py:116
  265.7 3.5 copy.119
  269.3 3.5 copy.120
  272.8 2.1 fusion.52
  276.4 1.9 collective-permute-start.2
  278.3 2.6 collective-permute-start.3
  283.3 4.4 collective-permute-done.3
  287.7 2.0 fusion.61
  291.1 2.1 gather_fusion
  294.6 7.5 %all-to-all-start.2 = ((bf16[32,8,4,768]{3,1,2,0:T(8,128)(2,1)}), bf16[32,8,4,768]{3,1,2,0:T(8,128)(2,1)S(1)}, u32[]{:S(2)}, u32[]{:S(2)}) async-start(bf16[32,8,4,768]{3,1,2,0:T(8,128)(2,1)} %copy.124), calls=%async_computation.2 | async-start | bytes 3145728 | tf_op jit(solution)/shard_map/all_to_all | solution.py:135
  302.3 142.3 %psum.7 = f32[768]{0:T(1024)} all-reduce(f32[768]{0:T(1024)S(1)} %reduce_sum.63), channel_id=1, replica_groups=mesh['dp'=16,'seq'=32] {'dp','seq'}, use_global_device_ids=true, to_apply=%region_16.17 | all-reduce | flops 768 | bytes 6144 | tf_op jit(solution)/shard_map/psum | solution.py:145
  (262 shorter events, 146.2 us)
Async XLA Ops:
  3.0 21.5 %copy-start.5 = (s32[128]{0:T(128)}, s32[128]{0:T(128)S(1)}, u32[]{:S(2)}) copy-start(s32[128]{0:T(128)S(1)} %fusion.65) | copy-start | bytes 1540
  5.4 28.5 %all-to-all-start = ((s32[32,1,8]{2,1,0:T(1,128)}), s32[32,1,8]{2,1,0:T(1,128)S(1)}, u32[]{:S(2)}, u32[]{:S(2)}) async-start(s32[32,1,8]{2,1,0:T(1,128)} %bitcast.5), calls=%async_computation | async-start | bytes 32768 | tf_op jit(solution)/shard_map/all_to_all | solution.py:78
  30.4 12.4 %copy-start.3 = (f32[768]{0:T(1024)S(1)}, f32[768]{0:T(1024)}, u32[]{:S(2)}) copy-start(f32[768]{0:T(1024)} %param.16) | copy-start | bytes 9220
  30.4 12.5 %copy-start.8 = (s32[1,4]{1,0:T(1,128)S(1)}, s32[1,4]{1,0:T(1,128)}, u32[]{:S(2)}) copy-start(s32[1,4]{1,0:T(1,128)} %param.19) | copy-start | bytes 52
  33.9 86.7 %all-to-all-start.1 = ((bf16[32,8,4,768]{3,1,2,0:T(8,128)(2,1)}), bf16[32,8,4,768]{3,1,2,0:T(8,128)(2,1)S(1)}, u32[]{:S(2)}, u32[]{:S(2)}) async-start(bf16[32,8,4,768]{3,1,2,0:T(8,128)(2,1)} %copy.103), calls=%async_computation.1 | async-start | bytes 3145728 | tf_op jit(solution)/shard_map/all_to_all | solution.py:84
  43.1 1.2 copy-start.9
  130.2 6.8 %collective-permute-start = (bf16[128,2,768]{2,1,0:T(2,128)(2,1)S(1)}, bf16[128,2,768]{2,1,0:T(2,128)(2,1)S(1)}, u32[]{:S(2)}, u32[]{:S(2)}) collective-permute-start(bf16[128,2,768]{2,1,0:T(2,128)(2,1)S(1)} %stack.15), channel_id=1, source_target_pairs={{0,1},{1,2},{2,3},{3,4},{4,5},{5,6},{6,7},{7,8},{8,9},{9,10},{10,1... | collective-permute-start | bytes 1179656 | tf_op jit(solution)/shard_map/ppermute | solution.py:16
  132.1 9.1 %collective-permute-start.1 = (bf16[128,2,768]{2,1,0:T(2,128)(2,1)S(1)}, bf16[128,2,768]{2,1,0:T(2,128)(2,1)S(1)}, u32[]{:S(2)}, u32[]{:S(2)}) collective-permute-start(bf16[128,2,768]{2,1,0:T(2,128)(2,1)S(1)} %stack.15), channel_id=1, source_target_pairs={{1,0},{2,1},{3,2},{4,3},{5,4},{6,5},{7,6},{8,7},{9,8},{10,9},{11,1... | collective-permute-start | bytes 1179656 | tf_op jit(solution)/shard_map/ppermute | solution.py:17
  148.7 0.8 copy-start.7
  148.7 0.8 copy-start.10
  148.7 0.8 copy-start.11
  274.9 6.0 %copy-start.4 = (s32[256,1]{0,1:T(1,128)S(1)}, s32[256,1]{0,1:T(1,128)}, u32[]{:S(2)}) copy-start(s32[256,1]{0,1:T(1,128)} %get-tuple-element.384) | copy-start | bytes 3076
  274.9 7.1 %copy-start.2 = (bf16[12,128,64]{1,2,0:T(8,128)(2,1)S(1)}, bf16[12,128,64]{1,2,0:T(8,128)(2,1)}, u32[]{:S(2)}) copy-start(bf16[12,128,64]{1,2,0:T(8,128)(2,1)} %get-tuple-element.650) | copy-start | bytes 589828
  276.4 6.9 %collective-permute-start.2 = (bf16[128,2,768]{2,1,0:T(2,128)(2,1)}, bf16[128,2,768]{2,1,0:T(2,128)(2,1)S(1)}, u32[]{:S(2)}, u32[]{:S(2)}) collective-permute-start(bf16[128,2,768]{2,1,0:T(2,128)(2,1)} %get-tuple-element.374), channel_id=1, source_target_pairs={{0,1},{1,2},{2,3},{3,4},{4,5},{5,6},{6,7},{7,8},{8,9},{9,10},{10,1... | collective-permute-start | bytes 1179656 | tf_op jit(solution)/shard_map/ppermute | solution.py:25
  278.3 9.4 %collective-permute-start.3 = (bf16[128,2,768]{2,1,0:T(2,128)(2,1)}, bf16[128,2,768]{2,1,0:T(2,128)(2,1)}, u32[]{:S(2)}, u32[]{:S(2)}) collective-permute-start(bf16[128,2,768]{2,1,0:T(2,128)(2,1)} %get-tuple-element.375), channel_id=1, source_target_pairs={{1,0},{2,1},{3,2},{4,3},{5,4},{6,5},{7,6},{8,7},{9,8},{10,9},{11,1... | collective-permute-start | bytes 1179656 | tf_op jit(solution)/shard_map/ppermute | solution.py:25
  283.1 6.6 %copy-start = (bf16[128,1,768]{2,1,0:T(2,128)(2,1)S(1)}, bf16[128,1,768]{2,1,0:T(2,128)(2,1)}, u32[]{:S(2)}) copy-start(bf16[128,1,768]{2,1,0:T(2,128)(2,1)} %copy.122) | copy-start | bytes 589828
  283.1 6.6 %copy-start.1 = (bf16[128,1,768]{2,1,0:T(2,128)(2,1)S(1)}, bf16[128,1,768]{2,1,0:T(2,128)(2,1)}, u32[]{:S(2)}) copy-start(bf16[128,1,768]{2,1,0:T(2,128)(2,1)} %copy.121) | copy-start | bytes 589828
  294.6 7.5 %copy-start.6 = (s32[128]{0:T(128)S(1)}, s32[128]{0:T(128)}, u32[]{:S(2)}) copy-start(s32[128]{0:T(128)} %copy-done.5) | copy-start | bytes 1540
  294.6 150.1 %all-to-all-start.2 = ((bf16[32,8,4,768]{3,1,2,0:T(8,128)(2,1)}), bf16[32,8,4,768]{3,1,2,0:T(8,128)(2,1)S(1)}, u32[]{:S(2)}, u32[]{:S(2)}) async-start(bf16[32,8,4,768]{3,1,2,0:T(8,128)(2,1)} %copy.124), calls=%async_computation.2 | async-start | bytes 3145728 | tf_op jit(solution)/shard_map/all_to_all | solution.py:135
where the time goes:
time: 455 us; the launch traced here: 450 us
  blocking collectives  142 us (31%)
  waiting for transfers between devices  87.2 us (19%)
  local copies, waits for them, and re-layouts  81.7 us (18%)
  matrix products  76.4 us (17%)
  starting transfers between devices  42.2 us (9%)
  other arithmetic  18.3 us (4%)
    psum x1, blocking collectives, body(): grad_bias = lax.psum(jnp.sum(dq_f, 0), ('dp', 'seq'))  142 us
    all_to_all x1, waiting for transfers between devices, body(): lax.all_to_all(buffer.reshape((peers, room) + stack.shape[1:]), 'seq', sp...  75 us
    dot_general x12, matrix products, head_backward(): lax.dot_general(ds, qh, (((0,), (0,)), ((), ())), preferred_element_type=...  19.1 us
    dot_general x12, matrix products, head_forward(): jnp.dot(p.astype(jnp.bfloat16), vh, preferred_element_type=jnp.float32)  18.6 us
    all_to_all x1, starting transfers between devices, body(): lax.all_to_all(marks, 'seq', split_axis=0, concat_axis=0, tiled=True)  16.8 us
    dynamic_update_slice x12, local copies, waits for them, and re-layouts, body(): lax.map(lambda a: head_forward(a[0], a[1], a[2], mask), (bq, bk, bv))  15.5 us
    dot_general x12, matrix products, head_forward(): lax.dot_general(qh, kh, (((1,), (1,)), ((), ())), preferred_element_type=...  12.4 us
    dot_general x12, matrix products, head_backward(): lax.dot_general(qh, kh, (((1,), (1,)), ((), ())), preferred_element_type=...  11.7 us
  transfers between devices with their start and end apart: 7, of which 5 were waited for; matrix products, arithmetic and copies ran while one was open for 3% of the time, Pallas kernels for 0%

commit v1 on v0

v1 whole, which is shorter than its diff:
```python
import jax
import jax.numpy as jnp
from jax import lax
from jax.experimental import pallas as pl
from jax.experimental.pallas import tpu as pltpu
from jax.sharding import PartitionSpec as P

HEAD_DIM = 64
ROWS = 128
WIDTH = 768
LANES = 128
CHUNKS = WIDTH // LANES
PEERS = 32
PACKS = 16
ROOM = 8
PAIRS = PEERS * 2 * ROOM
AHEAD = 3
MESH = pl.DeviceIdType.MESH
BF16 = jnp.bfloat16
F32 = jnp.float32


def dot(a, b):
    return jnp.dot(a, b, preferred_element_type=F32)


def dot_t(a, b):
    return lax.dot_general(a, b, (((1,), (1,)), ((), ())), preferred_element_type=F32)


def t_dot(a, b):
    return lax.dot_general(a, b, (((0,), (0,)), ((), ())), preferred_element_type=F32)


def iota(shape, dim):
    return lax.broadcasted_iota(jnp.int32, shape, dim)


def kernel(
    q_ref, k_ref, v_ref, g_ref, bias_ref, owner_ref, slot_ref, lengths_ref,
    o_out, dq_out, dk_out, dv_out, gb_out,
    pack, unpack, land, unland, live,
    marks_out, marks_in,
    sent, got, back_sent, back_got,
    kv, part_sent, part_got, own_parts, o_keep, dq_keep,
    gb, gb_seq, gb_pack, gb_dp,
    marks_ss, marks_rs, sent_s, got_s, back_ss, back_rs,
    kv_ss, kv_rs, part_ss, part_rs, seq_ss, seq_rs, dp_ss, dp_rs,
):
    dp = lax.axis_index("dp")
    me = lax.axis_index("seq")
    left = lax.rem(me + PEERS - 1, PEERS)
    right = lax.rem(me + 1, PEERS)

    barrier = pltpu.get_barrier_semaphore()

    def greet_seq(o, _):
        peer = lax.rem(me + o, PEERS)
        pl.semaphore_signal(barrier, inc=1, device_id=(dp, peer), device_id_type=MESH)
        return 0

    def greet_dp(o, _):
        peer = lax.rem(dp + o, PACKS)
        pl.semaphore_signal(barrier, inc=1, device_id=(peer, me), device_id_type=MESH)
        return 0

    lax.fori_loop(1, PEERS, greet_seq, 0)
    lax.fori_loop(1, PACKS, greet_dp, 0)

    owner = owner_ref[...]
    slot = slot_ref[...]
    to = (jnp.broadcast_to(owner, (PEERS, ROWS)) == iota((PEERS, ROWS), 0)).astype(F32)
    before = (iota((ROWS, ROWS), 0) < iota((ROWS, ROWS), 1)).astype(BF16)
    earlier = dot(to.astype(BF16), before)
    rank = jnp.sum(to * earlier, axis=0, keepdims=True).astype(jnp.int32)
    place = owner * (2 * ROOM) + rank
    places = jnp.concatenate([place, place + ROOM], axis=1)
    chosen = (jnp.broadcast_to(places, (PAIRS, 2 * ROWS)) == iota((PAIRS, 2 * ROWS), 0)).astype(F32)
    pack[...] = chosen.astype(BF16)
    unpack[...] = jnp.transpose(chosen).astype(BF16)
    ranked = jnp.where(
        jnp.broadcast_to(rank, (ROWS, ROWS)) == iota((ROWS, ROWS), 0),
        jnp.broadcast_to(slot + 1, (ROWS, ROWS)),
        0,
    ).astype(F32)
    marks = dot_t(to.astype(BF16), ranked.astype(BF16))
    for peer in range(PEERS):
        marks_out[peer] = marks[peer : peer + 1]
    marks_in[me] = marks_out[me]

    first = me * ROWS
    row_pos = first + iota((ROWS, 3 * ROWS), 0)
    col_pos = first - ROWS + iota((ROWS, 3 * ROWS), 1)
    row_seg = jnp.zeros((ROWS, 3 * ROWS), jnp.int32)
    col_seg = jnp.zeros((ROWS, 3 * ROWS), jnp.int32)
    end = jnp.int32(0)
    for utt in range(4):
        end = end + lengths_ref[0, utt]
        row_seg = row_seg + (row_pos >= end).astype(jnp.int32)
        col_seg = col_seg + (col_pos >= end).astype(jnp.int32)
    alive = (
        (jnp.abs(row_pos - col_pos) <= ROWS)
        & (row_seg == col_seg)
        & (col_pos >= 0)
        & (col_pos < PEERS * ROWS)
    )
    masked = jnp.where(alive, 0.0, -1e30).astype(F32)
    live[0:ROWS] = masked
    live[ROWS:] = masked
    gb[...] = jnp.zeros_like(gb)

    def lanes(c):
        return pl.ds(pl.multiple_of(c * LANES, LANES), LANES)

    def fill(c):
        x = jnp.concatenate(
            [
                jnp.concatenate([q_ref[:, lanes(c)], v_ref[:, lanes(c)]], axis=1),
                jnp.concatenate([k_ref[:, lanes(c)], g_ref[:, lanes(c)]], axis=1),
            ],
            axis=0,
        )
        packed = dot(pack[...], x).astype(BF16)
        sent[c] = packed.reshape(PEERS, 2 * ROOM, 2 * LANES)
        got[c, me] = sent[c, me]

    def send(c):
        def to_peer(o, _):
            peer = lax.rem(me + o, PEERS)
            pltpu.make_async_remote_copy(
                src_ref=sent.at[c, peer], dst_ref=got.at[c, me],
                send_sem=sent_s.at[c], recv_sem=got_s.at[c],
                device_id=(dp, peer), device_id_type=MESH,
            ).start()
            return 0

        lax.fori_loop(1, PEERS, to_peer, 0)

    def many(src, dst, send_sem, recv_sem, count):
        return pltpu.make_async_remote_copy(
            src_ref=src.at[pl.ds(0, count)], dst_ref=dst.at[pl.ds(0, count)],
            send_sem=send_sem, recv_sem=recv_sem,
            device_id=(dp, right), device_id_type=MESH,
        )

    def kv_copy(c, to_right):
        return pltpu.make_async_remote_copy(
            src_ref=kv.at[c, 1], dst_ref=kv.at[c, 0 if to_right else 2],
            send_sem=kv_ss.at[c, int(to_right)], recv_sem=kv_rs.at[c, int(to_right)],
            device_id=(dp, right if to_right else left), device_id_type=MESH,
        )

    def part_copy(c, to_right):
        side = int(to_right)
        return pltpu.make_async_remote_copy(
            src_ref=part_sent.at[c, side], dst_ref=part_got.at[c, side],
            send_sem=part_ss.at[c, side], recv_sem=part_rs.at[c, side],
            device_id=(dp, right if to_right else left), device_id_type=MESH,
        )

    fill(0)
    pl.semaphore_wait(barrier, PEERS - 1 + PACKS - 1)

    def send_marks(o, _):
        peer = lax.rem(me + o, PEERS)
        pltpu.make_async_remote_copy(
            src_ref=marks_out.at[peer], dst_ref=marks_in.at[me],
            send_sem=marks_ss, recv_sem=marks_rs,
            device_id=(dp, peer), device_id_type=MESH,
        ).start()
        return 0

    lax.fori_loop(1, PEERS, send_marks, 0)
    send(0)

    def early(c, _):
        fill(c)
        send(c)
        return 0

    lax.fori_loop(1, AHEAD, early, 0)

    many(marks_out, marks_in, marks_ss, marks_rs, PEERS - 1).wait_recv()
    arrived = jnp.concatenate([marks_in[peer] for peer in range(PEERS)], axis=0)
    spread = (iota((PAIRS, PEERS), 0) // (2 * ROOM) == iota((PAIRS, PEERS), 1)).astype(BF16)
    wide = dot(spread, arrived.astype(BF16))
    wide = jnp.where(iota((PAIRS, ROWS), 0) % ROOM == iota((PAIRS, ROWS), 1), wide, 0.0)
    mark = jnp.sum(wide, axis=1, keepdims=True).astype(jnp.int32)
    second = iota((PAIRS, 1), 0) % (2 * ROOM) // ROOM
    landing = jnp.where(mark > 0, mark - 1 + ROWS * second, -1)
    lands = (jnp.broadcast_to(landing, (PAIRS, 2 * ROWS)) == iota((PAIRS, 2 * ROWS), 1)).astype(F32)
    unland[...] = lands.astype(BF16)
    land[...] = jnp.transpose(lands).astype(BF16)

    low = iota((ROWS, LANES), 1) < HEAD_DIM

    def stacked(x):
        zero = jnp.zeros_like(x)
        return jnp.concatenate([jnp.where(low, x, zero), jnp.where(low, zero, x)], axis=0)

    def merged(x):
        return jnp.where(low, x[:ROWS], x[ROWS:])

    def arrive(c):
        many(sent.at[c], got.at[c], sent_s.at[c], got_s.at[c], PEERS - 1).wait_recv()
        x = dot(land[...], got[c].reshape(PAIRS, 2 * LANES))
        biased = (x[:ROWS, :LANES] + bias_ref[:, lanes(c)]).astype(BF16)
        o_keep[c] = biased
        dq_keep[c] = x[ROWS:, LANES:].astype(BF16)
        kv[c, 1, 0:ROWS] = x[ROWS:, :LANES].astype(BF16)
        kv[c, 1, ROWS:] = x[:ROWS, LANES:].astype(BF16)
        kv_copy(c, True).start()
        kv_copy(c, False).start()

    def attend(c):
        kv_copy(c, True).wait_recv()
        kv_copy(c, False).wait_recv()
        keys = jnp.concatenate([kv[c, side, 0:ROWS] for side in range(3)], axis=0)
        values = jnp.concatenate([kv[c, side, ROWS:] for side in range(3)], axis=0)
        b = stacked(o_keep[c].astype(F32)).astype(BF16)
        g32 = stacked(dq_keep[c].astype(F32))
        g = g32.astype(BF16)
        scale = 1.0 / HEAD_DIM**0.5
        s = dot_t(b, keys) * scale + live[...]
        top = jnp.max(s, axis=1, keepdims=True)
        e = jnp.exp(s - top)
        p = e * (1.0 / jnp.sum(e, axis=1, keepdims=True))
        prob = p.astype(BF16)
        o = merged(dot(prob, values)).astype(BF16)
        o32 = o.astype(F32)
        delta = jnp.sum(g32 * jnp.concatenate([o32, o32], axis=0), axis=1, keepdims=True)
        ds = (p * (dot_t(g, values) - delta) * scale).astype(BF16)
        dq = merged(dot(ds, keys))
        dk = t_dot(ds, b)
        dv = t_dot(prob, g)
        for side, at in ((0, 0), (1, 2 * ROWS)):
            part_sent[c, side, 0:ROWS] = dk[at : at + ROWS].astype(BF16)
            part_sent[c, side, ROWS:] = dv[at : at + ROWS].astype(BF16)
        part_copy(c, True).start()
        part_copy(c, False).start()
        own_parts[c, 0:ROWS] = dk[ROWS : 2 * ROWS]
        own_parts[c, ROWS:] = dv[ROWS : 2 * ROWS]
        o_keep[c] = o
        dq_keep[c] = dq.astype(BF16)
        gb[pl.ds(c, 1), :] = jnp.sum(dq, axis=0, keepdims=True)

    def give_back(c):
        part_copy(c, True).wait_recv()
        part_copy(c, False).wait_recv()
        total = own_parts[c] + part_got[c, 0].astype(F32) + part_got[c, 1].astype(F32)
        total = total.astype(BF16)
        x = jnp.concatenate(
            [
                jnp.concatenate([o_keep[c], total[:ROWS]], axis=1),
                jnp.concatenate([dq_keep[c], total[ROWS:]], axis=1),
            ],
            axis=0,
        )
        back_sent[c] = dot(unland[...], x).astype(BF16).reshape(PEERS, 2 * ROOM, 2 * LANES)
        back_got[c, me] = back_sent[c, me]

        def to_peer(o, _):
            peer = lax.rem(me + o, PEERS)
            pltpu.make_async_remote_copy(
                src_ref=back_sent.at[c, peer], dst_ref=back_got.at[c, me],
                send_sem=back_ss.at[c], recv_sem=back_rs.at[c],
                device_id=(dp, peer), device_id_type=MESH,
            ).start()
            return 0

        lax.fori_loop(1, PEERS, to_peer, 0)

    def finish(c):
        many(back_sent.at[c], back_got.at[c], back_ss.at[c], back_rs.at[c], PEERS - 1).wait_recv()
        x = dot(unpack[...], back_got[c].reshape(PAIRS, 2 * LANES)).astype(BF16)
        o_out[:, lanes(c)] = x[:ROWS, :LANES]
        dk_out[:, lanes(c)] = x[:ROWS, LANES:]
        dq_out[:, lanes(c)] = x[ROWS:, :LANES]
        dv_out[:, lanes(c)] = x[ROWS:, LANES:]

    def step(i, _):
        @pl.when(i + AHEAD < CHUNKS)
        def _():
            fill(i + AHEAD)
            send(i + AHEAD)

        @pl.when(i < CHUNKS)
        def _():
            arrive(i)

        @pl.when((i >= 1) & (i < CHUNKS + 1))
        def _():
            attend(i - 1)

        @pl.when(i >= 2)
        def _():
            give_back(i - 2)

        return 0

    lax.fori_loop(0, CHUNKS + 2, step, 0)

    gb_seq[me] = gb[...]

    def share_seq(o, _):
        peer = lax.rem(me + o, PEERS)
        pltpu.make_async_remote_copy(
            src_ref=gb, dst_ref=gb_seq.at[me],
            send_sem=seq_ss, recv_sem=seq_rs,
            device_id=(dp, peer), device_id_type=MESH,
        ).start()
        return 0

    lax.fori_loop(1, PEERS, share_seq, 0)

    def finish_one(c, _):
        finish(c)
        return 0

    lax.fori_loop(0, CHUNKS - 1, finish_one, 0)

    many(gb_seq, gb_seq, seq_ss, seq_rs, PEERS - 1).wait_recv()
    gb_pack[...] = jnp.sum(gb_seq[...], axis=0)
    gb_dp[dp] = gb_pack[...]

    def share_dp(o, _):
        peer = lax.rem(dp + o, PACKS)
        pltpu.make_async_remote_copy(
            src_ref=gb_pack, dst_ref=gb_dp.at[dp],
            send_sem=dp_ss, recv_sem=dp_rs,
            device_id=(peer, me), device_id_type=MESH,
        ).start()
        return 0

    lax.fori_loop(1, PACKS, share_dp, 0)
    finish(CHUNKS - 1)
    many(gb_dp, gb_dp, dp_ss, dp_rs, PACKS - 1).wait_recv()
    gb_out[...] = jnp.sum(gb_dp[...], axis=0)

    many(marks_out, marks_in, marks_ss, marks_rs, PEERS - 1).wait_send()
    many(gb_seq, gb_seq, seq_ss, seq_rs, PEERS - 1).wait_send()
    many(gb_dp, gb_dp, dp_ss, dp_rs, PACKS - 1).wait_send()

    def left_all(c, _):
        many(sent.at[c], got.at[c], sent_s.at[c], got_s.at[c], PEERS - 1).wait_send()
        many(back_sent.at[c], back_got.at[c], back_ss.at[c], back_rs.at[c], PEERS - 1).wait_send()
        for to_right in (True, False):
            kv_copy(c, to_right).wait_send()
            part_copy(c, to_right).wait_send()
        return 0

    lax.fori_loop(0, CHUNKS, left_all, 0)


def body(queries, keys, values, cotangent, pos_bias, owner, slot, lengths):
    vmem = pl.BlockSpec(memory_space=pltpu.VMEM)
    smem = pl.BlockSpec(memory_space=pltpu.SMEM)
    rows = jax.ShapeDtypeStruct((ROWS, WIDTH), BF16)
    dma = pltpu.SemaphoreType.DMA
    block = (CHUNKS, PEERS, 2 * ROOM, 2 * LANES)
    o, dq, dk, dv, gb = pl.pallas_call(
        kernel,
        out_shape=(rows, rows, rows, rows, jax.ShapeDtypeStruct((8, LANES), F32)),
        in_specs=[vmem] * 7 + [smem],
        out_specs=(vmem,) * 5,
        scratch_shapes=[
            pltpu.VMEM((PAIRS, 2 * ROWS), BF16),
            pltpu.VMEM((2 * ROWS, PAIRS), BF16),
            pltpu.VMEM((2 * ROWS, PAIRS), BF16),
            pltpu.VMEM((PAIRS, 2 * ROWS), BF16),
            pltpu.VMEM((2 * ROWS, 3 * ROWS), F32),
            pltpu.VMEM((PEERS, 1, LANES), F32),
            pltpu.VMEM((PEERS, 1, LANES), F32),
            pltpu.VMEM(block, BF16),
            pltpu.VMEM(block, BF16),
            pltpu.VMEM(block, BF16),
            pltpu.VMEM(block, BF16),
            pltpu.VMEM((CHUNKS, 3, 2 * ROWS, LANES), BF16),
            pltpu.VMEM((CHUNKS, 2, 2 * ROWS, LANES), BF16),
            pltpu.VMEM((CHUNKS, 2, 2 * ROWS, LANES), BF16),
            pltpu.VMEM((CHUNKS, 2 * ROWS, LANES), F32),
            pltpu.VMEM((CHUNKS, ROWS, LANES), BF16),
            pltpu.VMEM((CHUNKS, ROWS, LANES), BF16),
            pltpu.VMEM((8, LANES), F32),
            pltpu.VMEM((PEERS, 8, LANES), F32),
            pltpu.VMEM((8, LANES), F32),
            pltpu.VMEM((PACKS, 8, LANES), F32),
            dma, dma,
            dma((CHUNKS,)), dma((CHUNKS,)), dma((CHUNKS,)), dma((CHUNKS,)),
            dma((CHUNKS, 2)), dma((CHUNKS, 2)), dma((CHUNKS, 2)), dma((CHUNKS, 2)),
            dma, dma, dma, dma,
        ],
        compiler_params=pltpu.CompilerParams(
            collective_id=0, has_side_effects=True, vmem_limit_bytes=40 << 20
        ),
    )(
        queries[0], keys[0], values[0], cotangent[0],
        pos_bias[None, :], owner, slot, lengths,
    )
    return o[None], dq[None], dk[None], dv[None], gb[:CHUNKS].reshape(WIDTH)


def solution(mesh):
    rows = P("dp", "seq", None)
    in_specs = (rows, rows, rows, rows, P(), P("dp", "seq"), P("dp", "seq"), P("dp", None))
    out_specs = (rows, rows, rows, rows, P())
    return jax.shard_map(body, mesh=mesh, in_specs=in_specs, out_specs=out_specs, check_vma=False)
```

time: 455 us -> 186 us (0.41); the launches traced: 450 us -> 186 us
  Pallas kernels: 0 us -> 177 us
  blocking collectives: 142 us -> 0 us
  waiting for transfers between devices: 87.2 us -> 0 us
  matrix products: 76.4 us -> 0 us
  local copies, waits for them, and re-layouts: 81.7 us -> 8.37 us
  starting transfers between devices: 42.2 us -> 0 us
  other arithmetic: 18.3 us -> 0 us
    pallas_call x0 -> x1, Pallas kernels: none -> 177 us  [body(): pl.pallas_call(kernel, out_shape=(rows, rows, rows, rows, jax.ShapeDtypeS...]
    psum x1 -> x0, blocking collectives: 142 us -> none  [body(): grad_bias = lax.psum(jnp.sum(dq_f, 0), ('dp', 'seq'))]
    all_to_all x3 -> x0, waiting for transfers between devices: 78.4 us -> none  [the longest x1 75 us: body(): lax.all_to_all(buffer.reshape((peers, room) + stack.shape[1:]), 'seq', sp...]
    dot_general x84 -> x0, matrix products: 76.4 us -> none  [the longest x12 19.1 us: head_backward(): lax.dot_general(ds, qh, (((0,), (0,)), ((), ())), preferred_element_type=...]
    all_to_all x3 -> x0, starting transfers between devices: 33.1 us -> none  [the longest x1 16.8 us: body(): lax.all_to_all(marks, 'seq', split_axis=0, concat_axis=0, tiled=True)]
    dynamic_update_slice x12 -> x0, local copies, waits for them, and re-layouts: 15.5 us -> none  [body(): lax.map(lambda a: head_forward(a[0], a[1], a[2], mask), (bq, bk, bv))]
    scatter x3 -> x0, local copies, waits for them, and re-layouts: 13.1 us -> none  [the longest x1 7.64 us: body(): jnp.zeros((rows,) + flat.shape[1:], jnp.bfloat16).at[landing]]
    dynamic_slice x36 -> x0, local copies, waits for them, and re-layouts: 11.5 us -> none  [body(): lax.map(lambda a: head_forward(a[0], a[1], a[2], mask), (bq, bk, bv))]
  transfers between devices with their start and end apart: 7 -> 0, of which waited for: 5 -> 0; matrix products, arithmetic and copies ran while one was open for 3% -> 0% of each run, Pallas kernels for 0% -> 0%
where the time goes in v1:
time: 186 us
  Pallas kernels  177 us (95%)
  local copies, waits for them, and re-layouts  8.37 us (4%)
    pallas_call x1, Pallas kernels, body(): pl.pallas_call(kernel, out_shape=(rows, rows, rows, rows, jax.ShapeDtypeS...  177 us
    unnamed x20, local copies, waits for them, and re-layouts  7.77 us

profile of v1, /device:TPU:1, one launch (start us, length us, event | category | flops | bytes accessed | tf_op | source)
XLA Modules:
  0.0 186.0 jit_solution(16522448448428391861)
XLA Ops:
  0.6 0.0 copy-start.7
  0.6 0.7 copy-done.7
  1.3 0.0 copy-start.4
  1.3 0.0 copy-start.5
  1.3 0.0 copy-start.6
  1.3 0.6 copy-done.4
  2.0 0.0 copy-done.5
  2.0 0.0 copy-done.6
  2.0 0.0 copy-start
  2.0 0.9 copy-done
  2.9 0.0 copy-start.1
  2.9 0.9 copy-done.1
  3.9 0.0 copy-start.2
  3.9 0.9 copy-done.2
  4.8 0.0 copy-start.3
  4.8 0.9 copy-done.3
  5.7 176.9 %shard_map.119 = (bf16[128,768]{1,0:T(8,128)(2,1)S(1)}, bf16[128,768]{1,0:T(8,128)(2,1)S(1)}, bf16[128,768]{1,0:T(8,128)(2,1)S(1)}, bf16[128,768]{1,0:T(8,128)(2,1)S(1)}, f32[8,128]{1,0:T(8,128)S(1)}) custom-call(bf16[128,768]{1,0:T(8,128)(2,1)S(1)} %bitcast.14, bf16[128,768]{1,0:T(8,128)(2,1)S(1)} %bitcast.15, bf16[128,768]{1,0:T(8,128)(2,1)S(1)} %bitcast.16, ...), custom_call_target="tpu_custom_call" | custom-call | tf_op jit(solution)/shard_map/pallas_call | solution.py:361
  182.7 0.6 slice_bitcast_fusion
  183.3 0.7 copy.17
  183.9 0.7 copy.18
  184.6 0.7 copy.19
  185.3 0.7 copy.20
  (1 shorter events, 0.0 us)
Async XLA Ops:
  0.6 0.7 copy-start.7
  1.3 0.7 copy-start.4
  1.3 0.7 copy-start.5
  1.3 0.7 copy-start.6
  2.0 0.9 copy-start
  2.9 0.9 copy-start.1
  3.9 0.9 copy-start.2
  4.8 0.9 copy-start.3

commit v2 on v1

v2 whole, which is shorter than its diff:
```python
import jax
import jax.numpy as jnp
from jax import lax
from jax.experimental import pallas as pl
from jax.experimental.pallas import tpu as pltpu
from jax.sharding import PartitionSpec as P

HEAD_DIM = 64
ROWS = 128
WIDTH = 768
LANES = 128
WIDE = 256
CHUNKS = WIDTH // WIDE
PEERS = 32
PACKS = 16
ROOM = 8
PAIRS = PEERS * 2 * ROOM
MESH = pl.DeviceIdType.MESH
BF16 = jnp.bfloat16
F32 = jnp.float32


def dot(a, b):
    return jnp.dot(a, b, preferred_element_type=F32)


def dot_t(a, b):
    return lax.dot_general(a, b, (((1,), (1,)), ((), ())), preferred_element_type=F32)


def t_dot(a, b):
    return lax.dot_general(a, b, (((0,), (0,)), ((), ())), preferred_element_type=F32)


def iota(shape, dim):
    return lax.broadcasted_iota(jnp.int32, shape, dim)


def kernel(
    q_hbm, k_hbm, v_hbm, g_hbm, bias_hbm, owner_hbm, slot_hbm, lengths_hbm,
    o_hbm, dq_hbm, dk_hbm, dv_hbm, gb_out,
    x, y, pack, unpack, land, unland, live,
    marks_out, marks_in,
    sent, got, back_sent, back_got,
    kv, part_sent, part_got, own_parts, result,
    gb, gb_dp, gb_packs, gb_seq,
    bias_flat, bias, owner_ref, slot_ref, lengths_ref,
    small_s, in_s, out_s,
    marks_ss, marks_rs, sent_s, got_s, back_ss, back_rs,
    kv_ss, kv_rs, part_ss, part_rs, seq_ss, seq_rs, dp_ss, dp_rs,
):
    dp = lax.axis_index("dp")
    me = lax.axis_index("seq")
    left = lax.rem(me + PEERS - 1, PEERS)
    right = lax.rem(me + 1, PEERS)

    barrier = pltpu.get_barrier_semaphore()

    def greet_seq(o, _):
        peer = lax.rem(me + o, PEERS)
        pl.semaphore_signal(barrier, inc=1, device_id=(dp, peer), device_id_type=MESH)
        return 0

    def greet_dp(o, _):
        peer = lax.rem(dp + o, PACKS)
        pl.semaphore_signal(barrier, inc=1, device_id=(peer, me), device_id_type=MESH)
        return 0

    lax.fori_loop(1, PEERS, greet_seq, 0)
    lax.fori_loop(1, PACKS, greet_dp, 0)

    def wide(c):
        return pl.ds(pl.multiple_of(c * WIDE, WIDE), WIDE)

    small = [
        pltpu.make_async_copy(src, dst, small_s.at[i])
        for i, (src, dst) in enumerate(
            [
                (owner_hbm, owner_ref),
                (slot_hbm, slot_ref),
                (bias_hbm, bias_flat),
                (lengths_hbm, lengths_ref),
            ]
        )
    ]
    for copy in small:
        copy.start()

    inputs = (k_hbm, v_hbm, q_hbm, g_hbm)

    def load(array, c):
        return pltpu.make_async_copy(
            inputs[array].at[:, wide(c)],
            x.at[array // 2, c, pl.ds(array % 2 * ROWS, ROWS)],
            in_s.at[array, c],
        )

    for half in range(2):
        for c in range(CHUNKS):
            load(2 * half, c).start()
            load(2 * half + 1, c).start()

    for copy in small:
        copy.wait()
    owner = owner_ref[...]
    slot = slot_ref[...]
    to = (jnp.broadcast_to(owner, (PEERS, ROWS)) == iota((PEERS, ROWS), 0)).astype(F32)
    before = (iota((ROWS, ROWS), 0) < iota((ROWS, ROWS), 1)).astype(BF16)
    earlier = dot(to.astype(BF16), before)
    rank = jnp.sum(to * earlier, axis=0, keepdims=True).astype(jnp.int32)
    place = owner * (2 * ROOM) + rank
    places = jnp.concatenate([place, place + ROOM], axis=1)
    chosen = (jnp.broadcast_to(places, (PAIRS, 2 * ROWS)) == iota((PAIRS, 2 * ROWS), 0)).astype(F32)
    pack[...] = chosen.astype(BF16)

    def fill(half, c):
        load(2 * half, c).wait()
        load(2 * half + 1, c).wait()
        packed = dot(pack[...], x[half, c]).astype(BF16)
        sent[half, c] = packed.reshape(PEERS, 2 * ROOM, WIDE)
        got[half, c, me] = sent[half, c, me]

    def scatter(src, dst, send_sem, recv_sem):
        def to_peer(o, _):
            peer = lax.rem(me + 16 + (o // 2) * (1 - 2 * lax.rem(o, 2)) + PEERS, PEERS)
            pltpu.make_async_remote_copy(
                src_ref=src.at[peer], dst_ref=dst.at[me],
                send_sem=send_sem, recv_sem=recv_sem,
                device_id=(dp, peer), device_id_type=MESH,
            ).start()
            return 0

        lax.fori_loop(1, PEERS, to_peer, 0)

    def many(src, dst, send_sem, recv_sem, count=PEERS - 1):
        return pltpu.make_async_remote_copy(
            src_ref=src.at[pl.ds(0, count)], dst_ref=dst.at[pl.ds(0, count)],
            send_sem=send_sem, recv_sem=recv_sem,
            device_id=(dp, right), device_id_type=MESH,
        )

    def sending(half, c):
        return sent.at[half, c], got.at[half, c], sent_s.at[half, c], got_s.at[half, c]

    def returning(half, c):
        return back_sent.at[half, c], back_got.at[half, c], back_ss.at[half, c], back_rs.at[half, c]

    def kv_copy(c, to_right):
        return pltpu.make_async_remote_copy(
            src_ref=kv.at[c, 1], dst_ref=kv.at[c, 0 if to_right else 2],
            send_sem=kv_ss.at[c, int(to_right)], recv_sem=kv_rs.at[c, int(to_right)],
            device_id=(dp, right if to_right else left), device_id_type=MESH,
        )

    def part_copy(c, to_right):
        side = int(to_right)
        return pltpu.make_async_remote_copy(
            src_ref=part_sent.at[c, side], dst_ref=part_got.at[c, side],
            send_sem=part_ss.at[c, side], recv_sem=part_rs.at[c, side],
            device_id=(dp, right if to_right else left), device_id_type=MESH,
        )

    fill(0, 0)
    pl.semaphore_wait(barrier, PEERS - 1 + PACKS - 1)
    scatter(*sending(0, 0))

    ranked = jnp.where(
        jnp.broadcast_to(rank, (ROWS, ROWS)) == iota((ROWS, ROWS), 0),
        jnp.broadcast_to(slot + 1, (ROWS, ROWS)),
        0,
    ).astype(F32)
    marks = dot_t(to.astype(BF16), ranked.astype(BF16))
    for peer in range(PEERS):
        marks_out[peer] = marks[peer : peer + 1]
    marks_in[me] = marks_out[me]
    scatter(marks_out, marks_in, marks_ss, marks_rs)

    def early(c, _):
        fill(0, c)
        scatter(*sending(0, c))
        return 0

    lax.fori_loop(1, CHUNKS, early, 0)

    for c in range(CHUNKS):
        bias[c] = bias_flat[c * WIDE : (c + 1) * WIDE].reshape(1, WIDE)

    first = me * ROWS
    row_pos = first + iota((ROWS, 3 * ROWS), 0)
    col_pos = first - ROWS + iota((ROWS, 3 * ROWS), 1)
    row_seg = jnp.zeros((ROWS, 3 * ROWS), jnp.int32)
    col_seg = jnp.zeros((ROWS, 3 * ROWS), jnp.int32)
    end = jnp.int32(0)
    for utt in range(4):
        end = end + lengths_ref[0, utt]
        row_seg = row_seg + (row_pos >= end).astype(jnp.int32)
        col_seg = col_seg + (col_pos >= end).astype(jnp.int32)
    alive = (
        (jnp.abs(row_pos - col_pos) <= ROWS)
        & (row_seg == col_seg)
        & (col_pos >= 0)
        & (col_pos < PEERS * ROWS)
    )
    masked = jnp.where(alive, 0.0, -1e30).astype(F32)
    live[0:ROWS] = masked
    live[ROWS:] = masked
    gb[...] = jnp.zeros_like(gb)
    unpack[...] = jnp.transpose(pack[...].astype(F32)).astype(BF16)

    many(marks_out, marks_in, marks_ss, marks_rs).wait_recv()
    arrived = jnp.concatenate([marks_in[peer] for peer in range(PEERS)], axis=0)
    spread = (iota((PAIRS, PEERS), 0) // (2 * ROOM) == iota((PAIRS, PEERS), 1)).astype(BF16)
    copied = dot(spread, arrived.astype(BF16))
    copied = jnp.where(iota((PAIRS, ROWS), 0) % ROOM == iota((PAIRS, ROWS), 1), copied, 0.0)
    mark = jnp.sum(copied, axis=1, keepdims=True).astype(jnp.int32)
    second = iota((PAIRS, 1), 0) % (2 * ROOM) // ROOM
    landing = jnp.where(mark > 0, mark - 1 + ROWS * second, -1)
    lands = (jnp.broadcast_to(landing, (PAIRS, 2 * ROWS)) == iota((PAIRS, 2 * ROWS), 1)).astype(F32)
    unland[...] = lands.astype(BF16)
    land[...] = jnp.transpose(lands).astype(BF16)

    def arrive(half, c):
        many(*sending(half, c)).wait_recv()
        return dot(land[...], got[half, c].reshape(PAIRS, WIDE))

    def arrive_kv(c, _):
        kv[c, 1] = arrive(0, c).astype(BF16)
        kv_copy(c, True).start()
        kv_copy(c, False).start()
        fill(1, c)
        scatter(*sending(1, c))
        return 0

    lax.fori_loop(0, CHUNKS, arrive_kv, 0)

    low = iota((ROWS, LANES), 1) < HEAD_DIM
    scale = 1.0 / HEAD_DIM**0.5

    def stacked(a):
        zero = jnp.zeros_like(a)
        return jnp.concatenate([jnp.where(low, a, zero), jnp.where(low, zero, a)], axis=0)

    def merged(a):
        return jnp.where(low, a[:ROWS], a[ROWS:])

    def two_heads(c, sub):
        lanes = slice(sub * LANES, (sub + 1) * LANES)
        keys = jnp.concatenate([kv[c, side, 0:ROWS, lanes] for side in range(3)], axis=0)
        values = jnp.concatenate([kv[c, side, ROWS:, lanes] for side in range(3)], axis=0)
        b = stacked(y[0:ROWS, lanes]).astype(BF16)
        g32 = stacked(y[ROWS:, lanes])
        g = g32.astype(BF16)
        s = dot_t(b, keys) * scale + live[...]
        top = jnp.max(s, axis=1, keepdims=True)
        e = jnp.exp(s - top)
        p = e * (1.0 / jnp.sum(e, axis=1, keepdims=True))
        prob = p.astype(BF16)
        o = merged(dot(prob, values)).astype(BF16)
        o32 = o.astype(F32)
        delta = jnp.sum(g32 * jnp.concatenate([o32, o32], axis=0), axis=1, keepdims=True)
        ds = (p * (dot_t(g, values) - delta) * scale).astype(BF16)
        dq = merged(dot(ds, keys))
        dk = t_dot(ds, b)
        dv = t_dot(prob, g)
        for side, at in ((0, 0), (1, 2 * ROWS)):
            part_sent[c, side, 0:ROWS, lanes] = dk[at : at + ROWS].astype(BF16)
            part_sent[c, side, ROWS:, lanes] = dv[at : at + ROWS].astype(BF16)
        own_parts[c, 0:ROWS, lanes] = dk[ROWS : 2 * ROWS]
        own_parts[c, ROWS:, lanes] = dv[ROWS : 2 * ROWS]
        result[0:ROWS, lanes] = o
        result[ROWS:, lanes] = dq.astype(BF16)
        gb[pl.ds(2 * c + sub, 1), :] = jnp.sum(dq, axis=0, keepdims=True)

    def give_back(half, c, rows):
        back_sent[half, c] = dot(unland[...], rows).astype(BF16).reshape(PEERS, 2 * ROOM, WIDE)
        back_got[half, c, me] = back_sent[half, c, me]
        scatter(*returning(half, c))

    def give_parts(c):
        part_copy(c, True).wait_recv()
        part_copy(c, False).wait_recv()
        total = own_parts[c] + part_got[c, 0].astype(F32) + part_got[c, 1].astype(F32)
        give_back(1, c, total.astype(BF16))

    def share_packs(o, _):
        peer = lax.rem(dp + o, PACKS)
        pltpu.make_async_remote_copy(
            src_ref=gb, dst_ref=gb_dp.at[dp],
            send_sem=dp_ss, recv_sem=dp_rs,
            device_id=(peer, me), device_id_type=MESH,
        ).start()
        return 0

    def attend(c, _):
        qg = arrive(1, c)
        y[0:ROWS] = (qg[:ROWS] + bias[c]).astype(BF16).astype(F32)
        y[ROWS:] = qg[ROWS:]
        kv_copy(c, True).wait_recv()
        kv_copy(c, False).wait_recv()
        two_heads(c, 0)
        two_heads(c, 1)
        part_copy(c, True).start()
        part_copy(c, False).start()

        @pl.when(c == CHUNKS - 1)
        def _():
            gb_dp[dp] = gb[...]
            lax.fori_loop(1, PACKS, share_packs, 0)

        give_back(0, c, result[...])

        @pl.when(c >= 1)
        def _():
            give_parts(c - 1)

        return 0

    lax.fori_loop(0, CHUNKS, attend, 0)

    many(gb_dp, gb_dp, dp_ss, dp_rs, PACKS - 1).wait_recv()
    gb_packs[...] = jnp.sum(gb_dp[...], axis=0)
    gb_seq[me] = gb_packs[...]

    def share_seq(o, _):
        peer = lax.rem(me + o, PEERS)
        pltpu.make_async_remote_copy(
            src_ref=gb_packs, dst_ref=gb_seq.at[me],
            send_sem=seq_ss, recv_sem=seq_rs,
            device_id=(dp, peer), device_id_type=MESH,
        ).start()
        return 0

    lax.fori_loop(1, PEERS, share_seq, 0)
    give_parts(CHUNKS - 1)

    outputs = ((o_hbm, dq_hbm), (dk_hbm, dv_hbm))

    def store(half, row, c):
        return pltpu.make_async_copy(
            x.at[half, c, pl.ds(row * ROWS, ROWS)],
            outputs[half][row].at[:, wide(c)],
            out_s.at[half, row, c],
        )

    def finish(half, c):
        many(*returning(half, c)).wait_recv()
        x[half, c] = dot(unpack[...], back_got[half, c].reshape(PAIRS, WIDE)).astype(BF16)
        store(half, 0, c).start()
        store(half, 1, c).start()

    def finish_both(c, _):
        finish(0, c)
        finish(1, c)
        return 0

    lax.fori_loop(0, CHUNKS - 1, finish_both, 0)
    finish(0, CHUNKS - 1)
    many(gb_seq, gb_seq, seq_ss, seq_rs).wait_recv()
    total = jnp.sum(gb_seq[...], axis=0)
    for part in range(WIDTH // LANES):
        gb_out[:, part * LANES : (part + 1) * LANES] = total[part : part + 1]

    many(marks_out, marks_in, marks_ss, marks_rs).wait_send()
    many(gb_dp, gb_dp, dp_ss, dp_rs, PACKS - 1).wait_send()
    many(gb_seq, gb_seq, seq_ss, seq_rs).wait_send()

    def left_all(c, _):
        for half in range(2):
            many(*sending(half, c)).wait_send()
            many(*returning(half, c)).wait_send()
            kv_copy(c, half == 0).wait_send()
            part_copy(c, half == 0).wait_send()
        return 0

    lax.fori_loop(0, CHUNKS, left_all, 0)
    finish(1, CHUNKS - 1)

    def stored(c, _):
        for half in range(2):
            for row in range(2):
                store(half, row, c).wait()
        return 0

    lax.fori_loop(0, CHUNKS, stored, 0)


def copies(*refs):
    source, target, held = refs[0:5], refs[5:10], refs[10:15]
    flat, in_s, out_s = refs[15:]
    loads = [pltpu.make_async_copy(source[i], held[i], in_s.at[i]) for i in range(5)]
    stores = [pltpu.make_async_copy(held[i], target[i], out_s.at[i]) for i in range(4)]
    stores.append(pltpu.make_async_copy(flat, target[4], out_s.at[4]))
    for load in loads:
        load.start()
    for i in (4, 0, 1, 2, 3):
        loads[i].wait()
        if i == 4:
            flat[...] = held[4][...].reshape(WIDTH)
        stores[i].start()
    for store in stores:
        store.wait()


def body(queries, keys, values, cotangent, pos_bias, owner, slot, lengths):
    vmem = pl.BlockSpec(memory_space=pltpu.VMEM)
    hbm = pl.BlockSpec(memory_space=pltpu.HBM)
    rows = jax.ShapeDtypeStruct((ROWS, WIDTH), BF16)
    bias = jax.ShapeDtypeStruct((1, WIDTH), F32)
    dma = pltpu.SemaphoreType.DMA
    block = (2, CHUNKS, PEERS, 2 * ROOM, WIDE)
    sides = (CHUNKS, 2, 2 * ROWS, WIDE)
    results = pl.pallas_call(
        kernel,
        out_shape=(rows, rows, rows, rows, bias),
        in_specs=[hbm] * 8,
        out_specs=(hbm,) * 4 + (vmem,),
        scratch_shapes=[
            pltpu.VMEM((2, CHUNKS, 2 * ROWS, WIDE), BF16),
            pltpu.VMEM((2 * ROWS, WIDE), F32),
            pltpu.VMEM((PAIRS, 2 * ROWS), BF16),
            pltpu.VMEM((2 * ROWS, PAIRS), BF16),
            pltpu.VMEM((2 * ROWS, PAIRS), BF16),
            pltpu.VMEM((PAIRS, 2 * ROWS), BF16),
            pltpu.VMEM((2 * ROWS, 3 * ROWS), F32),
            pltpu.VMEM((PEERS, 1, LANES), F32),
            pltpu.VMEM((PEERS, 1, LANES), F32),
            pltpu.VMEM(block, BF16),
            pltpu.VMEM(block, BF16),
            pltpu.VMEM(block, BF16),
            pltpu.VMEM(block, BF16),
            pltpu.VMEM((CHUNKS, 3, 2 * ROWS, WIDE), BF16),
            pltpu.VMEM(sides, BF16),
            pltpu.VMEM(sides, BF16),
            pltpu.VMEM((CHUNKS, 2 * ROWS, WIDE), F32),
            pltpu.VMEM((2 * ROWS, WIDE), BF16),
            pltpu.VMEM((8, LANES), F32),
            pltpu.VMEM((PACKS, 8, LANES), F32),
            pltpu.VMEM((8, LANES), F32),
            pltpu.VMEM((PEERS, 8, LANES), F32),
            pltpu.VMEM((WIDTH,), F32),
            pltpu.VMEM((CHUNKS, 1, WIDE), F32),
            pltpu.VMEM((1, ROWS), jnp.int32),
            pltpu.VMEM((1, ROWS), jnp.int32),
            pltpu.SMEM((1, 4), jnp.int32),
            dma((4,)), dma((4, CHUNKS)), dma((2, 2, CHUNKS)),
            dma, dma,
            dma((2, CHUNKS)), dma((2, CHUNKS)), dma((2, CHUNKS)), dma((2, CHUNKS)),
            dma((CHUNKS, 2)), dma((CHUNKS, 2)), dma((CHUNKS, 2)), dma((CHUNKS, 2)),
            dma, dma, dma, dma,
        ],
        compiler_params=pltpu.CompilerParams(
            collective_id=0, has_side_effects=True, vmem_limit_bytes=60 << 20
        ),
    )(
        queries[0], keys[0], values[0], cotangent[0],
        pos_bias, owner, slot, lengths,
    )
    o, dq, dk, dv, gb = pl.pallas_call(
        copies,
        out_shape=(rows, rows, rows, rows, jax.ShapeDtypeStruct((WIDTH,), F32)),
        in_specs=[hbm] * 5,
        out_specs=(hbm,) * 5,
        scratch_shapes=[pltpu.VMEM((ROWS, WIDTH), BF16)] * 4
        + [pltpu.VMEM((1, WIDTH), F32), pltpu.VMEM((WIDTH,), F32), dma((5,)), dma((5,))],
        compiler_params=pltpu.CompilerParams(vmem_limit_bytes=60 << 20),
    )(*results)
    return o[None], dq[None], dk[None], dv[None], gb


def solution(mesh):
    rows = P("dp", "seq", None)
    in_specs = (rows, rows, rows, rows, P(), P("dp", "seq"), P("dp", "seq"), P("dp", None))
    out_specs = (rows, rows, rows, rows, P())
    return jax.shard_map(body, mesh=mesh, in_specs=in_specs, out_specs=out_specs, check_vma=False)
```

time: 186 us -> 174 us (0.935)
  local copies, waits for them, and re-layouts: 8.37 us -> 0 us
  Pallas kernels: 177 us -> 173 us
    unnamed x20 -> x0, local copies, waits for them, and re-layouts: 7.77 us -> none
    pallas_call x1 -> x2, Pallas kernels: 177 us -> 173 us  [the longest x1 171 us: body(): pl.pallas_call(kernel, out_shape=(rows, rows, rows, rows, bias), in_specs...]
where the time goes in v2:
time: 174 us; the launch traced here: 173 us
  Pallas kernels  173 us (99%)
    pallas_call x1, Pallas kernels, body(): pl.pallas_call(kernel, out_shape=(rows, rows, rows, rows, bias), in_specs...  171 us

profile of v2, /device:TPU:1, one launch (start us, length us, event | category | flops | bytes accessed | tf_op | source)
XLA Modules:
  0.0 173.3 jit_solution(9821278749415516835)
XLA Ops:
  0.6 170.7 %shard_map.119 = (bf16[128,768]{1,0:T(8,128)(2,1)}, bf16[128,768]{1,0:T(8,128)(2,1)}, bf16[128,768]{1,0:T(8,128)(2,1)}, bf16[128,768]{1,0:T(8,128)(2,1)}, f32[1,768]{1,0:T(1,128)}) custom-call(bf16[128,768]{1,0:T(8,128)(2,1)} %bitcast.8, bf16[128,768]{1,0:T(8,128)(2,1)} %bitcast.9, bf16[128,768]{1,0:T(8,128)(2,1)} %bitcast.10, bf16[128,768]{1,0:T(8,128)(2,1)} %bitcast.11, ...), custom_call_target="tpu_custom_call" | custom-call | tf_op jit(solution)/shard_map/pallas_call | solution.py:412
  171.3 2.0 %shard_map.120 = (bf16[128,768]{1,0:T(8,128)(2,1)}, bf16[128,768]{1,0:T(8,128)(2,1)}, bf16[128,768]{1,0:T(8,128)(2,1)}, bf16[128,768]{1,0:T(8,128)(2,1)}, f32[768]{0:T(1024)}) custom-call(bf16[128,768]{1,0:T(8,128)(2,1)} %get-tuple-element.15.refs_0_, bf16[128,768]{1,0:T(8,128)(2,1)} %get-tuple-element.16.refs_1_, ...), custom_call_target="tpu_custom_call" | custom-call | tf_op jit(solution)/shard_map/pallas_call | solution.py:458

commit v3 on v0

v3 whole, which is shorter than its diff:
```python
import jax
import jax.numpy as jnp
from jax import lax
from jax.experimental import pallas as pl
from jax.experimental.pallas import tpu as pltpu
from jax.sharding import PartitionSpec as P

HEADS = 12
HEAD_DIM = 64
ROWS = 128
WIDTH = HEADS * HEAD_DIM
LANES = 128
WIDE = 256
PAIRS = HEADS // 2
CHIPS = 16
PEERS = 32
PACKS = 16
FRAMES = PEERS * ROWS
HALF = FRAMES // 2
BASE = HALF - 2 * ROWS
HELD = HALF + 2 * ROWS
TALL = 256
GROUP = 4
MESH = pl.DeviceIdType.MESH
BF16 = jnp.bfloat16
F32 = jnp.float32


def dot(a, b):
    return jnp.dot(a, b, preferred_element_type=F32)


def dot_t(a, b):
    return lax.dot_general(a, b, (((1,), (1,)), ((), ())), preferred_element_type=F32)


def t_dot(a, b):
    return lax.dot_general(a, b, (((0,), (0,)), ((), ())), preferred_element_type=F32)


def iota(shape, dim):
    return lax.broadcasted_iota(jnp.int32, shape, dim)


def far_first(j):
    return lax.rem(CHIPS // 2 + (j + 1) // 2 * (2 * lax.rem(j, 2) - 1), CHIPS)


def chip_of(head):
    return head // 3 * 4 + head % 3


def kernel(
    q_hbm, k_hbm, v_hbm, g_hbm, bias_hbm, owner_hbm, slot_hbm, lengths_hbm,
    o_hbm, dq_hbm, dk_hbm, dv_hbm, gb_out,
    x, y, blocks, got, pos_out, pos_in, pos_row, pos_col,
    held, band, res, dkv, results, part_out, part_in, ret, back,
    bias_flat, bias, owner_ref, slot_ref, lengths_ref,
    gb, gb_dp, gb_packs, gb_seq,
    small_s, in_s, out_s,
    blocks_ss, got_rs, pos_ss, pos_rs, relay_ss, relay_rs,
    part_ss, part_rs, ret_ss, back_rs, seq_ss, seq_rs, dp_ss, dp_rs,
):
    dp = lax.axis_index("dp")
    me = lax.axis_index("seq")
    chip = me // 2
    core = lax.rem(me, 2)
    sibling = me + 1 - 2 * core
    active = lax.rem(chip, 4) < 3
    my_head = jnp.minimum(chip // 4 * 3 + lax.rem(chip, 4), HEADS - 1)

    barrier = pltpu.get_barrier_semaphore()

    def greet_seq(o, _):
        peer = lax.rem(me + o, PEERS)
        pl.semaphore_signal(barrier, inc=1, device_id=(dp, peer), device_id_type=MESH)
        return 0

    def greet_dp(o, _):
        peer = lax.rem(dp + o, PACKS)
        pl.semaphore_signal(barrier, inc=1, device_id=(peer, me), device_id_type=MESH)
        return 0

    lax.fori_loop(1, PEERS, greet_seq, 0)
    lax.fori_loop(1, PACKS, greet_dp, 0)

    inputs = (q_hbm, g_hbm, k_hbm, v_hbm)
    loads = [pltpu.make_async_copy(inputs[i], x.at[i], in_s.at[i]) for i in range(4)]
    small = [
        pltpu.make_async_copy(src, dst, small_s.at[i])
        for i, (src, dst) in enumerate(
            [
                (owner_hbm, owner_ref),
                (slot_hbm, slot_ref),
                (bias_hbm, bias_flat),
                (lengths_hbm, lengths_ref),
            ]
        )
    ]
    for copy in small + loads:
        copy.start()
    for copy in small:
        copy.wait()
    pos_out[...] = owner_ref[...] * ROWS + slot_ref[...]

    low = iota((ROWS, LANES), 1) < HEAD_DIM

    def swapped(a):
        return pltpu.roll(a, HEAD_DIM, 1)

    for copy in loads:
        copy.wait()
    for pair in range(PAIRS):
        lanes = slice(pair * LANES, (pair + 1) * LANES)
        q, g, k, v = (x[i, :, lanes].astype(F32) for i in range(4))
        for at, (a, b) in ((0, (q, g)), (LANES, (k, v))):
            blocks[2 * pair, :, at : at + LANES] = jnp.where(low, a, swapped(b)).astype(BF16)
            blocks[2 * pair + 1, :, at : at + LANES] = jnp.where(low, swapped(a), b).astype(BF16)

    def send_copy(head, j, peer):
        return pltpu.make_async_remote_copy(
            src_ref=blocks.at[head], dst_ref=got.at[j, core],
            send_sem=blocks_ss.at[j], recv_sem=got_rs.at[j],
            device_id=(dp, peer), device_id_type=MESH,
        )

    def relay_copy(j, part):
        return pltpu.make_async_remote_copy(
            src_ref=got.at[j, part], dst_ref=got.at[j, part],
            send_sem=relay_ss.at[j], recv_sem=relay_rs.at[j],
            device_id=(dp, sibling), device_id_type=MESH,
        )

    def part_copy(j):
        return pltpu.make_async_remote_copy(
            src_ref=part_out.at[j], dst_ref=part_in.at[j],
            send_sem=part_ss.at[j], recv_sem=part_rs.at[j],
            device_id=(dp, sibling), device_id_type=MESH,
        )

    def ret_copy(j, head, peer):
        return pltpu.make_async_remote_copy(
            src_ref=ret.at[j], dst_ref=back.at[head],
            send_sem=ret_ss.at[j], recv_sem=back_rs.at[head],
            device_id=(dp, peer), device_id_type=MESH,
        )

    def many(buf, send_sem, recv_sem, count):
        return pltpu.make_async_remote_copy(
            src_ref=buf.at[pl.ds(0, count)], dst_ref=buf.at[pl.ds(0, count)],
            send_sem=send_sem, recv_sem=recv_sem,
            device_id=(dp, sibling), device_id_type=MESH,
        )

    pl.semaphore_wait(barrier, PEERS - 1 + PACKS - 1)

    def send_pos(j, _):
        to = lax.rem(chip + far_first(j), CHIPS)

        def one(peer):
            pltpu.make_async_remote_copy(
                src_ref=pos_out, dst_ref=pos_in.at[2 * j + core],
                send_sem=pos_ss, recv_sem=pos_rs,
                device_id=(dp, peer), device_id_type=MESH,
            ).start()

        @pl.when(j < CHIPS - 1)
        def _():
            one(2 * to)
            one(2 * to + 1)

        @pl.when(j == CHIPS - 1)
        def _():
            one(sibling)

        return 0

    lax.fori_loop(0, CHIPS, send_pos, 0)
    pos_in[2 * CHIPS - 2 + core] = pos_out[...]

    def target(j):
        to = lax.rem(chip + far_first(j), CHIPS)
        return to, lax.rem(to, 4) < 3, jnp.minimum(to // 4 * 3 + lax.rem(to, 4), HEADS - 1)

    def send(j, _):
        to, has_head, head = target(j)

        @pl.when(has_head)
        def _():
            send_copy(head, j, 2 * to + core).start()

        return 0

    lax.fori_loop(0, CHIPS - 1, send, 0)

    many(pos_in, pos_ss, pos_rs, PEERS - 1).wait_recv()
    first = core * BASE

    @pl.when(active)
    def _():
        got[CHIPS - 1, core] = blocks[my_head]
        held[0:ROWS] = jnp.zeros((ROWS, WIDE), BF16)
        held[ROWS + HELD :] = jnp.zeros((ROWS, WIDE), BF16)
        dkv[...] = jnp.zeros_like(dkv)
        places = jnp.concatenate([pos_in[i] for i in range(PEERS)], axis=0)
        for i in range(PEERS // 8):
            pos_row[i] = jnp.concatenate([pos_in[8 * i + n] for n in range(8)], axis=1)
        pos_col[...] = jnp.transpose(
            jnp.concatenate([places, jnp.zeros((ROWS - PEERS, ROWS), jnp.int32)], axis=0).astype(F32)
        ).astype(jnp.int32)
        apart = iota((ROWS, 3 * ROWS), 0) - iota((ROWS, 3 * ROWS), 1) + ROWS
        band[...] = jnp.where(jnp.abs(apart) <= ROWS, 0.0, -1e30).astype(F32)
        for pair in range(PAIRS):
            bias[pair] = bias_flat[pair * LANES : (pair + 1) * LANES].reshape(1, LANES)

        def group(n, _):
            def take(j, _):
                @pl.when(j < CHIPS - 1)
                def _():
                    send_copy(0, j, sibling).wait_recv()

                relay_copy(j, core).start()
                return 0

            def taken(j, _):
                relay_copy(j, 1 - core).wait_recv()
                return 0

            lax.fori_loop(GROUP * n, GROUP * (n + 1), take, 0)
            lax.fori_loop(GROUP * n, GROUP * (n + 1), taken, 0)
            rows = got[pl.ds(GROUP * n, GROUP)].reshape(2 * GROUP * ROWS, WIDE)
            there = pos_row[n] - first

            def place(m, _):
                shape = (TALL, 2 * GROUP * ROWS)
                chosen = (jnp.broadcast_to(there - m * TALL, shape) == iota(shape, 0)).astype(F32)
                found = dot(chosen.astype(BF16), rows)
                at = pl.ds(pl.multiple_of(ROWS + m * TALL, ROWS), TALL)

                @pl.when(n == 0)
                def _():
                    held[at] = found.astype(BF16)

                @pl.when(n > 0)
                def _():
                    held[at] = (held[at].astype(F32) + found).astype(BF16)

                return 0

            lax.fori_loop(0, HELD // TALL, place, 0)
            return 0

        lax.fori_loop(0, CHIPS // GROUP, group, 0)

        pair_bias = bias[my_head // 2]
        head_bias = jnp.where(lax.rem(my_head, 2) == 1, swapped(pair_bias), pair_bias)
        head_bias = jnp.where(low[0:1], head_bias, 0.0)
        scale = 1.0 / HEAD_DIM**0.5

        def segment(pos):
            seg = jnp.zeros_like(pos)
            end = jnp.int32(0)
            for utt in range(4):
                end = end + lengths_ref[0, utt]
                seg = seg + (pos >= end).astype(jnp.int32)
            return seg

        def attend(i, total):
            start = pl.multiple_of((core + i) * ROWS, ROWS)
            at = pl.ds(pl.multiple_of(start + ROWS, ROWS), ROWS)
            window = pl.ds(start, 3 * ROWS)
            here = first + start
            row_pos = here + iota((ROWS, 1), 0)
            col_pos = here - ROWS + iota((1, 3 * ROWS), 1)
            row_seg = segment(row_pos)
            col_seg = jnp.where((col_pos >= 0) & (col_pos < FRAMES), segment(col_pos), -1)
            bg = (held[at, 0:LANES].astype(F32) + head_bias).astype(BF16).astype(F32)
            kv = held[window, LANES:]
            both = jnp.concatenate([jnp.where(low, bg, 0.0), jnp.where(low, 0.0, bg)], axis=0).astype(BF16)
            product = dot_t(both, kv)
            s = jnp.where(row_seg == col_seg, product[:ROWS] * scale + band[...], -1e30)
            top = jnp.max(s, axis=1, keepdims=True)
            e = jnp.exp(s - top)
            p = e * (1.0 / jnp.sum(e, axis=1, keepdims=True))
            prob = p.astype(BF16)
            o = dot(prob, kv).astype(BF16).astype(F32)
            delta = jnp.sum(jnp.where(low, 0.0, bg * o), axis=1, keepdims=True)
            ds = (p * (product[ROWS:] - delta) * scale).astype(BF16)
            dq = dot(ds, kv)
            res[at] = jnp.where(low, dq, o).astype(BF16)
            dkv[window] += t_dot(jnp.concatenate([ds, prob], axis=0), both)
            mine = (i + core >= 2 * core) & (i + core < HALF // ROWS + 2 * core)
            return total + jnp.where(mine, jnp.sum(dq, axis=0, keepdims=True), 0.0)

        gb[...] = lax.fori_loop(0, HALF // ROWS + 1, attend, jnp.zeros((1, LANES), F32))
        own = pl.ds(pl.multiple_of(ROWS + 2 * ROWS * core, ROWS), HALF)
        results[:, 0:LANES] = res[own]
        results[:, LANES:] = dkv[own].astype(BF16)

    @pl.when(jnp.logical_not(active))
    def _():
        gb[...] = jnp.zeros_like(gb)

    gb_dp[dp] = gb[...]

    def share_dp(o, _):
        peer = lax.rem(dp + o, PACKS)
        pltpu.make_async_remote_copy(
            src_ref=gb, dst_ref=gb_dp.at[dp],
            send_sem=dp_ss, recv_sem=dp_rs,
            device_id=(peer, me), device_id_type=MESH,
        ).start()
        return 0

    lax.fori_loop(1, PACKS, share_dp, 0)

    def source(j):
        return lax.rem(chip - far_first(j) + CHIPS, CHIPS)

    def make_parts(j):
        own_first = core * HALF
        lane = iota((ROWS, LANES), 1)
        cols = [
            jnp.sum(jnp.where(lane == 2 * j + n, pos_col[...], 0), axis=1, keepdims=True) - own_first
            for n in range(2)
        ]
        col = jnp.concatenate(cols, axis=0)
        shape = (2 * ROWS, HALF)
        chosen = (jnp.broadcast_to(col, shape) == iota(shape, 1)).astype(F32).astype(BF16)
        y[...] = dot(chosen, results[...]).astype(BF16)
        part_out[j] = y[pl.ds(pl.multiple_of((1 - core) * ROWS, ROWS), ROWS)]
        ret[j] = y[pl.ds(pl.multiple_of(core * ROWS, ROWS), ROWS)]
        part_copy(j).start()

    def give_back(j):
        part_copy(j).wait_recv()
        ret[j] = (ret[j].astype(F32) + part_in[j].astype(F32)).astype(BF16)

        @pl.when(j < CHIPS - 1)
        def _():
            ret_copy(j, my_head, 2 * source(j) + core).start()

        @pl.when(j == CHIPS - 1)
        def _():
            back[my_head] = ret[j]

    @pl.when(active)
    def _():
        def step(j, _):
            @pl.when(j < CHIPS)
            def _():
                make_parts(j)

            @pl.when(j >= 1)
            def _():
                give_back(j - 1)

            return 0

        lax.fori_loop(0, CHIPS + 1, step, 0)

    many(gb_dp, dp_ss, dp_rs, PACKS - 1).wait_recv()
    gb_packs[...] = jnp.sum(gb_dp[...], axis=0)
    gb_seq[me] = gb_packs[...]

    def share_seq(o, _):
        peer = lax.rem(me + o, PEERS)
        pltpu.make_async_remote_copy(
            src_ref=gb_packs, dst_ref=gb_seq.at[me],
            send_sem=seq_ss, recv_sem=seq_rs,
            device_id=(dp, peer), device_id_type=MESH,
        ).start()
        return 0

    lax.fori_loop(1, PEERS, share_seq, 0)

    outputs = (dq_hbm, o_hbm, dk_hbm, dv_hbm)

    def store(array, pair):
        lanes = slice(pair * LANES, (pair + 1) * LANES)
        return pltpu.make_async_copy(
            x.at[array, :, lanes], outputs[array].at[:, lanes], out_s.at[array, pair]
        )

    for pair in range(PAIRS):
        for head in (2 * pair, 2 * pair + 1):

            @pl.when(chip != chip_of(head))
            def _():
                ret_copy(0, head, sibling).wait_recv()

        lanes = slice(pair * LANES, (pair + 1) * LANES)
        for n in range(2):
            a = back[2 * pair, :, n * LANES : (n + 1) * LANES].astype(F32)
            b = back[2 * pair + 1, :, n * LANES : (n + 1) * LANES].astype(F32)
            x[2 * n, :, lanes] = jnp.where(low, a, swapped(b)).astype(BF16)
            x[2 * n + 1, :, lanes] = jnp.where(low, swapped(a), b).astype(BF16)
        for array in range(4):
            store(array, pair).start()

    many(gb_seq, seq_ss, seq_rs, PEERS - 1).wait_recv()
    for pair in range(PAIRS):
        a, b = (
            gb_seq[2 * chip_of(head)] + gb_seq[2 * chip_of(head) + 1]
            for head in (2 * pair, 2 * pair + 1)
        )
        gb_out[:, pair * LANES : (pair + 1) * LANES] = jnp.where(low[0:1], a, swapped(b))

    many(pos_in, pos_ss, pos_rs, PEERS - 1).wait_send()
    many(gb_dp, dp_ss, dp_rs, PACKS - 1).wait_send()
    many(gb_seq, seq_ss, seq_rs, PEERS - 1).wait_send()

    def left(j, _):
        to, has_head, head = target(j)

        @pl.when(has_head & (j < CHIPS - 1))
        def _():
            send_copy(head, j, 2 * to + core).wait_send()

        @pl.when(active)
        def _():
            relay_copy(j, core).wait_send()
            part_copy(j).wait_send()

            @pl.when(j < CHIPS - 1)
            def _():
                ret_copy(j, my_head, 2 * source(j) + core).wait_send()

        return 0

    lax.fori_loop(0, CHIPS, left, 0)
    for pair in range(PAIRS):
        for array in range(4):
            store(array, pair).wait()


def copies(*refs):
    source, target, held = refs[0:5], refs[5:10], refs[10:15]
    flat, in_s, out_s = refs[15:]
    loads = [pltpu.make_async_copy(source[i], held[i], in_s.at[i]) for i in range(5)]
    stores = [pltpu.make_async_copy(held[i], target[i], out_s.at[i]) for i in range(4)]
    stores.append(pltpu.make_async_copy(flat, target[4], out_s.at[4]))
    for load in loads:
        load.start()
    for i in (4, 0, 1, 2, 3):
        loads[i].wait()
        if i == 4:
            flat[...] = held[4][...].reshape(WIDTH)
        stores[i].start()
    for move in stores:
        move.wait()


def body(queries, keys, values, cotangent, pos_bias, owner, slot, lengths):
    vmem = pl.BlockSpec(memory_space=pltpu.VMEM)
    hbm = pl.BlockSpec(memory_space=pltpu.HBM)
    rows = jax.ShapeDtypeStruct((ROWS, WIDTH), BF16)
    row = jax.ShapeDtypeStruct((1, WIDTH), F32)
    dma = pltpu.SemaphoreType.DMA
    i32 = jnp.int32
    results = pl.pallas_call(
        kernel,
        out_shape=(rows, rows, rows, rows, row),
        in_specs=[hbm] * 8,
        out_specs=(hbm,) * 4 + (vmem,),
        scratch_shapes=[
            pltpu.VMEM((4, ROWS, WIDTH), BF16),
            pltpu.VMEM((2 * ROWS, WIDE), BF16),
            pltpu.VMEM((HEADS, ROWS, WIDE), BF16),
            pltpu.VMEM((CHIPS, 2, ROWS, WIDE), BF16),
            pltpu.VMEM((1, ROWS), i32),
            pltpu.VMEM((PEERS, 1, ROWS), i32),
            pltpu.VMEM((PEERS // 8, 1, 8 * ROWS), i32),
            pltpu.VMEM((ROWS, LANES), i32),
            pltpu.VMEM((HELD + 2 * ROWS, WIDE), BF16),
            pltpu.VMEM((ROWS, 3 * ROWS), F32),
            pltpu.VMEM((HELD + 2 * ROWS, LANES), BF16),
            pltpu.VMEM((HELD + 2 * ROWS, LANES), F32),
            pltpu.VMEM((HALF, WIDE), BF16),
            pltpu.VMEM((CHIPS, ROWS, WIDE), BF16),
            pltpu.VMEM((CHIPS, ROWS, WIDE), BF16),
            pltpu.VMEM((CHIPS, ROWS, WIDE), BF16),
            pltpu.VMEM((HEADS, ROWS, WIDE), BF16),
            pltpu.VMEM((WIDTH,), F32),
            pltpu.VMEM((PAIRS, 1, LANES), F32),
            pltpu.VMEM((1, ROWS), i32),
            pltpu.VMEM((1, ROWS), i32),
            pltpu.SMEM((1, 4), i32),
            pltpu.VMEM((1, LANES), F32),
            pltpu.VMEM((PACKS, 1, LANES), F32),
            pltpu.VMEM((1, LANES), F32),
            pltpu.VMEM((PEERS, 1, LANES), F32),
            dma((4,)), dma((4,)), dma((4, PAIRS)),
            dma((CHIPS,)), dma((CHIPS,)), dma, dma, dma((CHIPS,)), dma((CHIPS,)),
            dma((CHIPS,)), dma((CHIPS,)), dma((CHIPS,)), dma((HEADS,)),
            dma, dma, dma, dma,
        ],
        compiler_params=pltpu.CompilerParams(
            collective_id=0, has_side_effects=True, vmem_limit_bytes=60 << 20
        ),
    )(
        queries[0], keys[0], values[0], cotangent[0],
        pos_bias, owner, slot, lengths,
    )
    o, dq, dk, dv, gb = pl.pallas_call(
        copies,
        out_shape=(rows, rows, rows, rows, jax.ShapeDtypeStruct((WIDTH,), F32)),
        in_specs=[hbm] * 5,
        out_specs=(hbm,) * 5,
        scratch_shapes=[pltpu.VMEM((ROWS, WIDTH), BF16)] * 4
        + [pltpu.VMEM((1, WIDTH), F32), pltpu.VMEM((WIDTH,), F32), dma((5,)), dma((5,))],
        compiler_params=pltpu.CompilerParams(vmem_limit_bytes=60 << 20),
    )(*results)
    return o[None], dq[None], dk[None], dv[None], gb


def solution(mesh):
    rows = P("dp", "seq", None)
    in_specs = (rows, rows, rows, rows, P(), P("dp", "seq"), P("dp", "seq"), P("dp", None))
    out_specs = (rows, rows, rows, rows, P())
    return jax.shard_map(body, mesh=mesh, in_specs=in_specs, out_specs=out_specs, check_vma=False)
```

time: 455 us -> 137 us (0.30)
  blocking collectives: 142 us -> 0 us
  Pallas kernels: 0 us -> 136 us
  waiting for transfers between devices: 87.2 us -> 0 us
  local copies, waits for them, and re-layouts: 81.7 us -> 0 us
  matrix products: 76.4 us -> 0 us
  starting transfers between devices: 42.2 us -> 0 us
  other arithmetic: 18.3 us -> 0 us
    psum x1 -> x0, blocking collectives: 142 us -> none  [body(): grad_bias = lax.psum(jnp.sum(dq_f, 0), ('dp', 'seq'))]
    pallas_call x0 -> x2, Pallas kernels: none -> 136 us  [the longest x1 134 us: body(): pl.pallas_call(kernel, out_shape=(rows, rows, rows, rows, row), in_specs=...]
    all_to_all x3 -> x0, waiting for transfers between devices: 78.4 us -> none  [the longest x1 75 us: body(): lax.all_to_all(buffer.reshape((peers, room) + stack.shape[1:]), 'seq', sp...]
    dot_general x84 -> x0, matrix products: 76.4 us -> none  [the longest x12 19.1 us: head_backward(): lax.dot_general(ds, qh, (((0,), (0,)), ((), ())), preferred_element_type=...]
    all_to_all x3 -> x0, starting transfers between devices: 33.1 us -> none  [the longest x1 16.8 us: body(): lax.all_to_all(marks, 'seq', split_axis=0, concat_axis=0, tiled=True)]
    dynamic_update_slice x12 -> x0, local copies, waits for them, and re-layouts: 15.5 us -> none  [body(): lax.map(lambda a: head_forward(a[0], a[1], a[2], mask), (bq, bk, bv))]
    scatter x3 -> x0, local copies, waits for them, and re-layouts: 13.1 us -> none  [the longest x1 7.64 us: body(): jnp.zeros((rows,) + flat.shape[1:], jnp.bfloat16).at[landing]]
    dynamic_slice x36 -> x0, local copies, waits for them, and re-layouts: 11.5 us -> none  [body(): lax.map(lambda a: head_forward(a[0], a[1], a[2], mask), (bq, bk, bv))]
  transfers between devices with their start and end apart: 7 -> 0, of which waited for: 5 -> 0; matrix products, arithmetic and copies ran while one was open for 3% -> 0% of each run, Pallas kernels for 0% -> 0%
where the time goes in v3:
time: 137 us; the launch traced here: 136 us
  Pallas kernels  136 us (99%)
    pallas_call x1, Pallas kernels, body(): pl.pallas_call(kernel, out_shape=(rows, rows, rows, rows, row), in_specs=...  134 us

profile of v3, /device:TPU:1, one launch (start us, length us, event | category | flops | bytes accessed | tf_op | source)
XLA Modules:
  0.0 136.5 jit_solution(5962584838712105385)
XLA Ops:
  0.6 133.9 %shard_map.119 = (bf16[128,768]{1,0:T(8,128)(2,1)}, bf16[128,768]{1,0:T(8,128)(2,1)}, bf16[128,768]{1,0:T(8,128)(2,1)}, bf16[128,768]{1,0:T(8,128)(2,1)}, f32[1,768]{1,0:T(1,128)}) custom-call(bf16[128,768]{1,0:T(8,128)(2,1)} %bitcast.8, bf16[128,768]{1,0:T(8,128)(2,1)} %bitcast.9, bf16[128,768]{1,0:T(8,128)(2,1)} %bitcast.10, bf16[128,768]{1,0:T(8,128)(2,1)} %bitcast.11, ...), custom_call_target="tpu_custom_call" | custom-call | tf_op jit(solution)/shard_map/pallas_call | solution.py:461
  134.5 2.0 %shard_map.120 = (bf16[128,768]{1,0:T(8,128)(2,1)}, bf16[128,768]{1,0:T(8,128)(2,1)}, bf16[128,768]{1,0:T(8,128)(2,1)}, bf16[128,768]{1,0:T(8,128)(2,1)}, f32[768]{0:T(1024)}) custom-call(bf16[128,768]{1,0:T(8,128)(2,1)} %get-tuple-element.15.refs_0_, bf16[128,768]{1,0:T(8,128)(2,1)} %get-tuple-element.16.refs_1_, ...), custom_call_target="tpu_custom_call" | custom-call | tf_op jit(solution)/shard_map/pallas_call | solution.py:505

commit v4 on v3

--- a/solution.py
+++ b/solution.py
@@ -21,6 +21,7 @@
 HELD = HALF + 2 * ROWS
 TALL = 256
 GROUP = 4
+SELF = 1
 MESH = pl.DeviceIdType.MESH
 BF16 = jnp.bfloat16
 F32 = jnp.float32
@@ -42,8 +43,12 @@
     return lax.broadcasted_iota(jnp.int32, shape, dim)
 
 
-def far_first(j):
-    return lax.rem(CHIPS // 2 + (j + 1) // 2 * (2 * lax.rem(j, 2) - 1), CHIPS)
+def wrapped(at, size):
+    return jnp.where(at >= size, at - size, at)
+
+
+def offset(group, at):
+    return (8, CHIPS, 1, 9)[at] + (-1, -1, 1, 1)[at] * group
 
 
 def chip_of(head):
@@ -53,13 +58,14 @@
 def kernel(
     q_hbm, k_hbm, v_hbm, g_hbm, bias_hbm, owner_hbm, slot_hbm, lengths_hbm,
     o_hbm, dq_hbm, dk_hbm, dv_hbm, gb_out,
-    x, y, blocks, got, pos_out, pos_in, pos_row, pos_col,
+    x, y, blocks, got, pos_out, pos_in, pos_col,
     held, band, res, dkv, results, part_out, part_in, ret, back,
     bias_flat, bias, owner_ref, slot_ref, lengths_ref,
-    gb, gb_dp, gb_packs, gb_seq,
+    gb, gb_dp, gb_half, gb_other, gb_head, gb_heads,
     small_s, in_s, out_s,
     blocks_ss, got_rs, pos_ss, pos_rs, relay_ss, relay_rs,
-    part_ss, part_rs, ret_ss, back_rs, seq_ss, seq_rs, dp_ss, dp_rs,
+    part_ss, part_rs, ret_ss, back_rs, heads_ss, heads_rs, dp_ss, dp_rs,
+    relay_pos_ss, relay_pos_rs, half_ss, half_rs,
 ):
     dp = lax.axis_index("dp")
     me = lax.axis_index("seq")
@@ -119,14 +125,14 @@
 
     def send_copy(head, j, peer):
         return pltpu.make_async_remote_copy(
-            src_ref=blocks.at[head], dst_ref=got.at[j, core],
+            src_ref=blocks.at[head], dst_ref=got.at[core, j],
             send_sem=blocks_ss.at[j], recv_sem=got_rs.at[j],
             device_id=(dp, peer), device_id_type=MESH,
         )
 
     def relay_copy(j, part):
         return pltpu.make_async_remote_copy(
-            src_ref=got.at[j, part], dst_ref=got.at[j, part],
+            src_ref=got.at[part, j], dst_ref=got.at[part, j],
             send_sem=relay_ss.at[j], recv_sem=relay_rs.at[j],
             device_id=(dp, sibling), device_id_type=MESH,
         )
@@ -154,103 +160,119 @@
 
     pl.semaphore_wait(barrier, PEERS - 1 + PACKS - 1)
 
-    def send_pos(j, _):
-        to = lax.rem(chip + far_first(j), CHIPS)
-
-        def one(peer):
-            pltpu.make_async_remote_copy(
-                src_ref=pos_out, dst_ref=pos_in.at[2 * j + core],
-                send_sem=pos_ss, recv_sem=pos_rs,
-                device_id=(dp, peer), device_id_type=MESH,
-            ).start()
-
-        @pl.when(j < CHIPS - 1)
-        def _():
-            one(2 * to)
-            one(2 * to + 1)
-
-        @pl.when(j == CHIPS - 1)
-        def _():
-            one(sibling)
-
-        return 0
-
-    lax.fori_loop(0, CHIPS, send_pos, 0)
-    pos_in[2 * CHIPS - 2 + core] = pos_out[...]
-
-    def target(j):
-        to = lax.rem(chip + far_first(j), CHIPS)
-        return to, lax.rem(to, 4) < 3, jnp.minimum(to // 4 * 3 + lax.rem(to, 4), HEADS - 1)
-
-    def send(j, _):
-        to, has_head, head = target(j)
-
-        @pl.when(has_head)
-        def _():
-            send_copy(head, j, 2 * to + core).start()
-
-        return 0
-
-    lax.fori_loop(0, CHIPS - 1, send, 0)
-
-    many(pos_in, pos_ss, pos_rs, PEERS - 1).wait_recv()
+    def pos_copy(j, peer):
+        return pltpu.make_async_remote_copy(
+            src_ref=pos_out, dst_ref=pos_in.at[core, j],
+            send_sem=pos_ss.at[j], recv_sem=pos_rs.at[j],
+            device_id=(dp, peer), device_id_type=MESH,
+        )
+
+    def relay_pos(n, part):
+        rows = pl.ds(GROUP * n, GROUP)
+        return pltpu.make_async_remote_copy(
+            src_ref=pos_in.at[part, rows], dst_ref=pos_in.at[part, rows],
+            send_sem=relay_pos_ss.at[n], recv_sem=relay_pos_rs.at[n],
+            device_id=(dp, sibling), device_id_type=MESH,
+        )
+
+    half_copy = pltpu.make_async_remote_copy(
+        src_ref=gb_half, dst_ref=gb_other,
+        send_sem=half_ss, recv_sem=half_rs,
+        device_id=(dp, sibling), device_id_type=MESH,
+    )
+
+    eighth = lax.rem(chip, 8)
+
+    def each_sent(turn, act, begin=0, end=CHIPS):
+        for j in range(begin, end):
+            if j == SELF:
+                continue
+            off = offset(j // GROUP, j % GROUP) % CHIPS
+            to = wrapped(chip + off, CHIPS)
+            at = wrapped(eighth + off % 8, 8)
+            first_turn = (at == 0) | (at == 2) | (at == 5)
+            second_turn = (at == 1) | (at == 4) | (at == 6)
+            skipped = sum((to >= 4 * n).astype(jnp.int32) for n in (1, 2, 3))
+
+            @pl.when(second_turn if turn else first_turn)
+            def _():
+                act(pos_copy(j, 2 * to + core))
+                act(send_copy(jnp.minimum(to - skipped, HEADS - 1), j, 2 * to + core))
+
+    def start(copy):
+        copy.start()
+
+    def left(copy):
+        copy.wait_send()
+
+    early = (eighth == 0) | (eighth == 2) | (eighth == 5)
+    each_sent(0, start)
+
+    @pl.when(jnp.logical_not(early))
+    def _():
+        each_sent(0, left)
+        each_sent(1, start)
+
     first = core * BASE
 
     @pl.when(active)
     def _():
-        got[CHIPS - 1, core] = blocks[my_head]
+        got[core, SELF] = blocks[my_head]
+        pos_in[core, SELF] = pos_out[...]
         held[0:ROWS] = jnp.zeros((ROWS, WIDE), BF16)
         held[ROWS + HELD :] = jnp.zeros((ROWS, WIDE), BF16)
         dkv[...] = jnp.zeros_like(dkv)
-        places = jnp.concatenate([pos_in[i] for i in range(PEERS)], axis=0)
-        for i in range(PEERS // 8):
-            pos_row[i] = jnp.concatenate([pos_in[8 * i + n] for n in range(8)], axis=1)
-        pos_col[...] = jnp.transpose(
-            jnp.concatenate([places, jnp.zeros((ROWS - PEERS, ROWS), jnp.int32)], axis=0).astype(F32)
-        ).astype(jnp.int32)
         apart = iota((ROWS, 3 * ROWS), 0) - iota((ROWS, 3 * ROWS), 1) + ROWS
         band[...] = jnp.where(jnp.abs(apart) <= ROWS, 0.0, -1e30).astype(F32)
         for pair in range(PAIRS):
             bias[pair] = bias_flat[pair * LANES : (pair + 1) * LANES].reshape(1, LANES)
 
-        def group(n, _):
-            def take(j, _):
-                @pl.when(j < CHIPS - 1)
-                def _():
-                    send_copy(0, j, sibling).wait_recv()
-
-                relay_copy(j, core).start()
-                return 0
-
-            def taken(j, _):
-                relay_copy(j, 1 - core).wait_recv()
-                return 0
-
-            lax.fori_loop(GROUP * n, GROUP * (n + 1), take, 0)
-            lax.fori_loop(GROUP * n, GROUP * (n + 1), taken, 0)
-            rows = got[pl.ds(GROUP * n, GROUP)].reshape(2 * GROUP * ROWS, WIDE)
-            there = pos_row[n] - first
+        def put(n, part, fresh):
+            rows = got[part, pl.ds(GROUP * n, GROUP)].reshape(GROUP * ROWS, WIDE)
+            there = jnp.concatenate([pos_in[part, GROUP * n + i] for i in range(GROUP)], axis=1) - first
+            shape = (TALL, GROUP * ROWS)
 
             def place(m, _):
-                shape = (TALL, 2 * GROUP * ROWS)
                 chosen = (jnp.broadcast_to(there - m * TALL, shape) == iota(shape, 0)).astype(F32)
                 found = dot(chosen.astype(BF16), rows)
                 at = pl.ds(pl.multiple_of(ROWS + m * TALL, ROWS), TALL)
-
-                @pl.when(n == 0)
+                if not fresh:
+                    found = found + held[at].astype(F32)
+                held[at] = found.astype(BF16)
+                return 0
+
+            lax.fori_loop(0, HELD // TALL, place, 0)
+
+        def take(j, _):
+            @pl.when(j != SELF)
+            def _():
+                pos_copy(j, sibling).wait_recv()
+                send_copy(0, j, sibling).wait_recv()
+
+            relay_copy(j, core).start()
+            return 0
+
+        def taken(j, _):
+            relay_copy(j, 1 - core).wait_recv()
+            return 0
+
+        for n in range(CHIPS // GROUP):
+            lax.fori_loop(GROUP * n, GROUP * (n + 1), take, 0)
+            relay_pos(n, core).start()
+            if n == 1:
+
+                @pl.when(early)
                 def _():
-                    held[at] = found.astype(BF16)
-
-                @pl.when(n > 0)
-                def _():
-                    held[at] = (held[at].astype(F32) + found).astype(BF16)
-
-                return 0
-
-            lax.fori_loop(0, HELD // TALL, place, 0)
-            return 0
-
-        lax.fori_loop(0, CHIPS // GROUP, group, 0)
+                    each_sent(1, start)
+
+            put(n, core, n == 0)
+            lax.fori_loop(GROUP * n, GROUP * (n + 1), taken, 0)
+            relay_pos(n, 1 - core).wait_recv()
+            put(n, 1 - core, False)
+
+        places = [pos_in[part, j] for part in range(2) for j in range(CHIPS)]
+        places = jnp.concatenate(places + [jnp.zeros((ROWS - PEERS, ROWS), jnp.int32)], axis=0)
+        pos_col[...] = jnp.transpose(places.astype(F32)).astype(jnp.int32)
 
         pair_bias = bias[my_head // 2]
         head_bias = jnp.where(lax.rem(my_head, 2) == 1, swapped(pair_bias), pair_bias)
@@ -265,7 +287,7 @@
                 seg = seg + (pos >= end).astype(jnp.int32)
             return seg
 
-        def attend(i, total):
+        def unit(i):
             start = pl.multiple_of((core + i) * ROWS, ROWS)
             at = pl.ds(pl.multiple_of(start + ROWS, ROWS), ROWS)
             window = pl.ds(start, 3 * ROWS)
@@ -274,36 +296,45 @@
             col_pos = here - ROWS + iota((1, 3 * ROWS), 1)
             row_seg = segment(row_pos)
             col_seg = jnp.where((col_pos >= 0) & (col_pos < FRAMES), segment(col_pos), -1)
-            bg = (held[at, 0:LANES].astype(F32) + head_bias).astype(BF16).astype(F32)
+            bg = (held[at, 0:LANES].astype(F32) + head_bias).astype(BF16).astype(F32) * scale
             kv = held[window, LANES:]
             both = jnp.concatenate([jnp.where(low, bg, 0.0), jnp.where(low, 0.0, bg)], axis=0).astype(BF16)
             product = dot_t(both, kv)
-            s = jnp.where(row_seg == col_seg, product[:ROWS] * scale + band[...], -1e30)
+            s = jnp.where(row_seg == col_seg, product[:ROWS] + band[...], -1e30)
             top = jnp.max(s, axis=1, keepdims=True)
             e = jnp.exp(s - top)
             p = e * (1.0 / jnp.sum(e, axis=1, keepdims=True))
             prob = p.astype(BF16)
             o = dot(prob, kv).astype(BF16).astype(F32)
             delta = jnp.sum(jnp.where(low, 0.0, bg * o), axis=1, keepdims=True)
-            ds = (p * (product[ROWS:] - delta) * scale).astype(BF16)
+            ds = (p * (product[ROWS:] - delta)).astype(BF16)
             dq = dot(ds, kv)
-            res[at] = jnp.where(low, dq, o).astype(BF16)
-            dkv[window] += t_dot(jnp.concatenate([ds, prob], axis=0), both)
             mine = (i + core >= 2 * core) & (i + core < HALF // ROWS + 2 * core)
-            return total + jnp.where(mine, jnp.sum(dq, axis=0, keepdims=True), 0.0)
-
-        gb[...] = lax.fori_loop(0, HALF // ROWS + 1, attend, jnp.zeros((1, LANES), F32))
+            return (
+                at,
+                window,
+                jnp.where(low, dq, o).astype(BF16),
+                t_dot(jnp.concatenate([ds, prob], axis=0), both),
+                jnp.where(mine, jnp.sum(dq, axis=0, keepdims=True), 0.0),
+            )
+
+        def attend(units):
+            made = [unit(i) for i in units]
+            for at, window, rows, grads, _ in made:
+                res[at] = rows
+                dkv[window] += grads
+            return sum(dq for _, _, _, _, dq in made)
+
+        units = HALF // ROWS // 2
+        total = lax.fori_loop(
+            0, units, lambda i, total: total + attend((i, i + units)), jnp.zeros((1, LANES), F32)
+        )
+        gb[...] = total + attend((2 * units,))
         own = pl.ds(pl.multiple_of(ROWS + 2 * ROWS * core, ROWS), HALF)
         results[:, 0:LANES] = res[own]
-        results[:, LANES:] = dkv[own].astype(BF16)
-
-    @pl.when(jnp.logical_not(active))
-    def _():
-        gb[...] = jnp.zeros_like(gb)
-
-    gb_dp[dp] = gb[...]
-
-    def share_dp(o, _):
+        results[:, LANES:] = (dkv[own] * (1.0 / scale)).astype(BF16)
+
+    def share_packs(o, _):
         peer = lax.rem(dp + o, PACKS)
         pltpu.make_async_remote_copy(
             src_ref=gb, dst_ref=gb_dp.at[dp],
@@ -312,16 +343,14 @@
         ).start()
         return 0
 
-    lax.fori_loop(1, PACKS, share_dp, 0)
-
-    def source(j):
-        return lax.rem(chip - far_first(j) + CHIPS, CHIPS)
+    def source(group, at):
+        return wrapped(chip - offset(group, at) + CHIPS, CHIPS)
 
     def make_parts(j):
         own_first = core * HALF
         lane = iota((ROWS, LANES), 1)
         cols = [
-            jnp.sum(jnp.where(lane == 2 * j + n, pos_col[...], 0), axis=1, keepdims=True) - own_first
+            jnp.sum(jnp.where(lane == CHIPS * n + j, pos_col[...], 0), axis=1, keepdims=True) - own_first
             for n in range(2)
         ]
         col = jnp.concatenate(cols, axis=0)
@@ -332,47 +361,67 @@
         ret[j] = y[pl.ds(pl.multiple_of(core * ROWS, ROWS), ROWS)]
         part_copy(j).start()
 
-    def give_back(j):
+    def give_back(group, at):
+        j = GROUP * group + at
         part_copy(j).wait_recv()
         ret[j] = (ret[j].astype(F32) + part_in[j].astype(F32)).astype(BF16)
 
-        @pl.when(j < CHIPS - 1)
-        def _():
-            ret_copy(j, my_head, 2 * source(j) + core).start()
-
-        @pl.when(j == CHIPS - 1)
-        def _():
+        def to_source():
+            ret_copy(j, my_head, 2 * source(group, at) + core).start()
+
+        def to_self():
             back[my_head] = ret[j]
 
+        if at == SELF:
+            pl.when(group != 0)(to_source)
+            pl.when(group == 0)(to_self)
+        else:
+            to_source()
+
+    def share_head():
+        for j in range(CHIPS):
+            if j != SELF:
+                pltpu.make_async_remote_copy(
+                    src_ref=gb_head, dst_ref=gb_heads.at[my_head],
+                    send_sem=heads_ss, recv_sem=heads_rs,
+                    device_id=(dp, 2 * source(j // GROUP, j % GROUP) + core), device_id_type=MESH,
+                ).start()
+
     @pl.when(active)
     def _():
-        def step(j, _):
-            @pl.when(j < CHIPS)
-            def _():
-                make_parts(j)
-
-            @pl.when(j >= 1)
-            def _():
-                give_back(j - 1)
+        def step(group, _):
+            make_parts(GROUP * group)
+
+            @pl.when(group >= 1)
+            def _():
+                give_back(group - 1, GROUP - 1)
+
+            for at in range(1, GROUP):
+                make_parts(GROUP * group + at)
+                give_back(group, at - 1)
+
+            @pl.when(group == 0)
+            def _():
+                gb_dp[dp] = gb[...]
+                lax.fori_loop(1, PACKS, share_packs, 0)
+
+            @pl.when(group == 1)
+            def _():
+                many(gb_dp, dp_ss, dp_rs, PACKS - 1).wait_recv()
+                gb_half[...] = jnp.sum(gb_dp[...], axis=0)
+                half_copy.start()
+
+            @pl.when(group == 2)
+            def _():
+                half_copy.wait_recv()
+                gb_head[...] = gb_half[...] + gb_other[...]
+                gb_heads[my_head] = gb_head[...]
+                share_head()
 
             return 0
 
-        lax.fori_loop(0, CHIPS + 1, step, 0)
-
-    many(gb_dp, dp_ss, dp_rs, PACKS - 1).wait_recv()
-    gb_packs[...] = jnp.sum(gb_dp[...], axis=0)
-    gb_seq[me] = gb_packs[...]
-
-    def share_seq(o, _):
-        peer = lax.rem(me + o, PEERS)
-        pltpu.make_async_remote_copy(
-            src_ref=gb_packs, dst_ref=gb_seq.at[me],
-            send_sem=seq_ss, recv_sem=seq_rs,
-            device_id=(dp, peer), device_id_type=MESH,
-        ).start()
-        return 0
-
-    lax.fori_loop(1, PEERS, share_seq, 0)
+        lax.fori_loop(0, CHIPS // GROUP, step, 0)
+        give_back(CHIPS // GROUP - 1, GROUP - 1)
 
     outputs = (dq_hbm, o_hbm, dk_hbm, dv_hbm)
 
@@ -398,37 +447,46 @@
         for array in range(4):
             store(array, pair).start()
 
-    many(gb_seq, seq_ss, seq_rs, PEERS - 1).wait_recv()
+    @pl.when(active)
+    def _():
+        many(gb_heads, heads_ss, heads_rs, HEADS - 1).wait_recv()
+
+    @pl.when(jnp.logical_not(active))
+    def _():
+        many(gb_heads, heads_ss, heads_rs, HEADS).wait_recv()
+
     for pair in range(PAIRS):
-        a, b = (
-            gb_seq[2 * chip_of(head)] + gb_seq[2 * chip_of(head) + 1]
-            for head in (2 * pair, 2 * pair + 1)
-        )
+        a, b = gb_heads[2 * pair], gb_heads[2 * pair + 1]
         gb_out[:, pair * LANES : (pair + 1) * LANES] = jnp.where(low[0:1], a, swapped(b))
 
-    many(pos_in, pos_ss, pos_rs, PEERS - 1).wait_send()
-    many(gb_dp, dp_ss, dp_rs, PACKS - 1).wait_send()
-    many(gb_seq, seq_ss, seq_rs, PEERS - 1).wait_send()
-
-    def left(j, _):
-        to, has_head, head = target(j)
-
-        @pl.when(has_head & (j < CHIPS - 1))
+    @pl.when(active)
+    def _():
+        many(gb_dp, dp_ss, dp_rs, PACKS - 1).wait_send()
+        many(gb_dp, heads_ss, heads_rs, CHIPS - 1).wait_send()
+        half_copy.wait_send()
+        for n in range(CHIPS // GROUP):
+            relay_pos(n, core).wait_send()
+
+    @pl.when(early)
+    def _():
+        each_sent(0, left)
+
+    each_sent(1, left)
+
+    def given(j, _):
+        relay_copy(j, core).wait_send()
+        part_copy(j).wait_send()
+
+        @pl.when(j != SELF)
         def _():
-            send_copy(head, j, 2 * to + core).wait_send()
-
-        @pl.when(active)
-        def _():
-            relay_copy(j, core).wait_send()
-            part_copy(j).wait_send()
-
-            @pl.when(j < CHIPS - 1)
-            def _():
-                ret_copy(j, my_head, 2 * source(j) + core).wait_send()
+            ret_copy(j, my_head, sibling).wait_send()
 
         return 0
 
-    lax.fori_loop(0, CHIPS, left, 0)
+    @pl.when(active)
+    def _():
+        lax.fori_loop(0, CHIPS, given, 0)
+
     for pair in range(PAIRS):
         for array in range(4):
             store(array, pair).wait()
@@ -467,10 +525,9 @@
             pltpu.VMEM((4, ROWS, WIDTH), BF16),
             pltpu.VMEM((2 * ROWS, WIDE), BF16),
             pltpu.VMEM((HEADS, ROWS, WIDE), BF16),
-            pltpu.VMEM((CHIPS, 2, ROWS, WIDE), BF16),
+            pltpu.VMEM((2, CHIPS, ROWS, WIDE), BF16),
             pltpu.VMEM((1, ROWS), i32),
-            pltpu.VMEM((PEERS, 1, ROWS), i32),
-            pltpu.VMEM((PEERS // 8, 1, 8 * ROWS), i32),
+            pltpu.VMEM((2, CHIPS, 1, ROWS), i32),
             pltpu.VMEM((ROWS, LANES), i32),
             pltpu.VMEM((HELD + 2 * ROWS, WIDE), BF16),
             pltpu.VMEM((ROWS, 3 * ROWS), F32),
@@ -489,11 +546,14 @@
             pltpu.VMEM((1, LANES), F32),
             pltpu.VMEM((PACKS, 1, LANES), F32),
             pltpu.VMEM((1, LANES), F32),
-            pltpu.VMEM((PEERS, 1, LANES), F32),
+            pltpu.VMEM((1, LANES), F32),
+            pltpu.VMEM((1, LANES), F32),
+            pltpu.VMEM((HEADS, 1, LANES), F32),
             dma((4,)), dma((4,)), dma((4, PAIRS)),
-            dma((CHIPS,)), dma((CHIPS,)), dma, dma, dma((CHIPS,)), dma((CHIPS,)),
+            dma((CHIPS,)), dma((CHIPS,)), dma((CHIPS,)), dma((CHIPS,)), dma((CHIPS,)), dma((CHIPS,)),
             dma((CHIPS,)), dma((CHIPS,)), dma((CHIPS,)), dma((HEADS,)),
             dma, dma, dma, dma,
+            dma((GROUP,)), dma((GROUP,)), dma, dma,
         ],
         compiler_params=pltpu.CompilerParams(
             collective_id=0, has_side_effects=True, vmem_limit_bytes=60 << 20

time: 137 us -> 126 us (0.920)
  Pallas kernels: 136 us -> 125 us
    pallas_call x1, Pallas kernels: 134 us -> 123 us  [body(): pl.pallas_call(kernel, out_shape=(rows, rows, rows, rows, row), in_specs=...]
where the time goes in v4:
time: 126 us; the launch traced here: 125 us
  Pallas kernels  125 us (99%)
    pallas_call x1, Pallas kernels, body(): pl.pallas_call(kernel, out_shape=(rows, rows, rows, rows, row), in_specs=...  123 us

profile of v4, /device:TPU:1, one launch (start us, length us, event | category | flops | bytes accessed | tf_op | source)
XLA Modules:
  0.0 125.4 jit_solution(14088033641578983660)
XLA Ops:
  0.6 122.8 %shard_map.119 = (bf16[128,768]{1,0:T(8,128)(2,1)}, bf16[128,768]{1,0:T(8,128)(2,1)}, bf16[128,768]{1,0:T(8,128)(2,1)}, bf16[128,768]{1,0:T(8,128)(2,1)}, f32[1,768]{1,0:T(1,128)}) custom-call(bf16[128,768]{1,0:T(8,128)(2,1)} %bitcast.8, bf16[128,768]{1,0:T(8,128)(2,1)} %bitcast.9, bf16[128,768]{1,0:T(8,128)(2,1)} %bitcast.10, bf16[128,768]{1,0:T(8,128)(2,1)} %bitcast.11, ...), custom_call_target="tpu_custom_call" | custom-call | tf_op jit(solution)/shard_map/pallas_call | solution.py:519
  123.4 2.0 %shard_map.120 = (bf16[128,768]{1,0:T(8,128)(2,1)}, bf16[128,768]{1,0:T(8,128)(2,1)}, bf16[128,768]{1,0:T(8,128)(2,1)}, bf16[128,768]{1,0:T(8,128)(2,1)}, f32[768]{0:T(1024)}) custom-call(bf16[128,768]{1,0:T(8,128)(2,1)} %get-tuple-element.15.refs_0_, bf16[128,768]{1,0:T(8,128)(2,1)} %get-tuple-element.16.refs_1_, ...), custom_call_target="tpu_custom_call" | custom-call | tf_op jit(solution)/shard_map/pallas_call | solution.py:565

commit v5 on v4

--- a/solution.py
+++ b/solution.py
@@ -19,7 +19,7 @@
 HALF = FRAMES // 2
 BASE = HALF - 2 * ROWS
 HELD = HALF + 2 * ROWS
-TALL = 256
+TALL = 768
 GROUP = 4
 SELF = 1
 MESH = pl.DeviceIdType.MESH
@@ -405,13 +405,13 @@
                 gb_dp[dp] = gb[...]
                 lax.fori_loop(1, PACKS, share_packs, 0)
 
-            @pl.when(group == 1)
+            @pl.when(group == 2)
             def _():
                 many(gb_dp, dp_ss, dp_rs, PACKS - 1).wait_recv()
                 gb_half[...] = jnp.sum(gb_dp[...], axis=0)
                 half_copy.start()
 
-            @pl.when(group == 2)
+            @pl.when(group == 3)
             def _():
                 half_copy.wait_recv()
                 gb_head[...] = gb_half[...] + gb_other[...]

time: 126 us -> 120 us (0.952)
  Pallas kernels: 125 us -> 119 us
    pallas_call x1, Pallas kernels: 123 us -> 117 us  [body(): pl.pallas_call(kernel, out_shape=(rows, rows, rows, rows, row), in_specs=...]
where the time goes in v5:
time: 120 us
  Pallas kernels  119 us (99%)
    pallas_call x1, Pallas kernels, body(): pl.pallas_call(kernel, out_shape=(rows, rows, rows, rows, row), in_specs=...  117 us

profile of v5, /device:TPU:1, one launch (start us, length us, event | category | flops | bytes accessed | tf_op | source)
XLA Modules:
  0.0 119.9 jit_solution(423960449275153824)
XLA Ops:
  0.6 117.3 %shard_map.119 = (bf16[128,768]{1,0:T(8,128)(2,1)}, bf16[128,768]{1,0:T(8,128)(2,1)}, bf16[128,768]{1,0:T(8,128)(2,1)}, bf16[128,768]{1,0:T(8,128)(2,1)}, f32[1,768]{1,0:T(1,128)}) custom-call(bf16[128,768]{1,0:T(8,128)(2,1)} %bitcast.8, bf16[128,768]{1,0:T(8,128)(2,1)} %bitcast.9, bf16[128,768]{1,0:T(8,128)(2,1)} %bitcast.10, bf16[128,768]{1,0:T(8,128)(2,1)} %bitcast.11, ...), custom_call_target="tpu_custom_call" | custom-call | tf_op jit(solution)/shard_map/pallas_call | solution.py:519
  117.9 2.0 %shard_map.120 = (bf16[128,768]{1,0:T(8,128)(2,1)}, bf16[128,768]{1,0:T(8,128)(2,1)}, bf16[128,768]{1,0:T(8,128)(2,1)}, bf16[128,768]{1,0:T(8,128)(2,1)}, f32[768]{0:T(1024)}) custom-call(bf16[128,768]{1,0:T(8,128)(2,1)} %get-tuple-element.15.refs_0_, bf16[128,768]{1,0:T(8,128)(2,1)} %get-tuple-element.16.refs_1_, ...), custom_call_target="tpu_custom_call" | custom-call | tf_op jit(solution)/shard_map/pallas_call | solution.py:565
